TPU v7x, 32 devices: a whole 2x2x4 slice. The times are simulated.
32 devices in a mesh: dp: 8 (over z, x), section: 2 (over core), tensor: 2 (over y).
Axes of the slice: x: 2, y: 2, z: 4, core: 2. Of those that a mesh axis runs over, the one named last changes fastest.
Arguments:
- source_tokens: bfloat16 [4096, 4096], P('dp'), may hold values from -6 to 6
- destination: int32 [4096], P('dp'), may hold values from -1 to 7, as said below
- segment_ids: int32 [4096], P('dp'), may hold values from -1 to 4095, as said below
- positions: int32 [4096], P('dp'), may hold values from 0 to 63, as said below
- norm_gain: float32 [2, 4096], P('section'), may hold values from 0.1 to 1.9
- w_query: bfloat16 [2, 4096, 4096], P('section', 'dp', 'tensor')
- w_key: bfloat16 [2, 4096, 1024], P('section', 'dp', 'tensor')
- w_value: bfloat16 [2, 4096, 1024], P('section', 'dp', 'tensor'), may hold values from -0.09375 to 0.09375
- w_out: bfloat16 [2, 4096, 4096], P('section', 'tensor', 'dp'), may hold values from -0.09375 to 0.09375
Outputs:
- final_states: bfloat16 [4096, 4096], P(('dp', 'section', 'tensor'))
Inputs may be any that keep to these rules, and one draw needn't show every extreme that they name: `destination`: -1 marks an empty source row, otherwise the receiving replica. A device's rows that name one replica stand together in order and hold whole sequences; at most 64 of a device's rows name one replica, and in every draw one replica receives exactly 64 from every device. `segment_ids`: equal for the tokens of one sequence and different between sequences anywhere; -1 on empty rows. `positions`: 0 at a sequence's first token and rising by one along it; 0 on empty rows.
All inputs are finite; a program needn't handle non-finite values.
Results may differ from a plain program's by a relative error of at most 0.015.
Values may be sent and summed in bfloat16 or wider, within the bound.
A program may use at most 192 MiB of HBM per device.

v0:
```python
import jax
import jax.numpy as jnp
from jax import lax
from jax.sharding import PartitionSpec as P

HEAD_DIM = 128


THETA = 500000.0
EPSILON = 1e-05


def shifted(array, axis, by):
    count = lax.axis_size(axis)
    pairs = [(i, i + by) for i in range(count) if 0 <= i + by < count]
    return lax.ppermute(array, axis, pairs)


def spread(value, axis, source):
    kept = jnp.where(lax.axis_index(axis) == source, value, 0).astype(value.dtype)
    return lax.psum(kept, axis)


def rotate(values, places):
    half_dim = HEAD_DIM // 2
    frequency = THETA ** (-(jnp.arange(half_dim, dtype=jnp.float32) * 2.0) / HEAD_DIM)
    angles = places.astype(jnp.float32)[..., None] * frequency
    cosine = jnp.concatenate([jnp.cos(angles), jnp.cos(angles)], axis=-1)[..., None, :]
    sine_part = jnp.concatenate([jnp.sin(angles), jnp.sin(angles)], axis=-1)[..., None, :]
    turned = jnp.concatenate([-values[..., half_dim:], values[..., :half_dim]], axis=-1)
    return values * cosine + turned * sine_part


def normalize(residual, gain_row):
    widened = residual.astype(jnp.float32)
    inv_scale = lax.rsqrt(jnp.mean(widened * widened, axis=-1, keepdims=True) + EPSILON)
    return (widened * inv_scale * gain_row).astype(jnp.bfloat16)


def attend_local(projected, id_row, pos_row, query_width, key_width):
    row_len = projected.shape[0]
    q_heads = query_width // HEAD_DIM
    kv_heads = key_width // HEAD_DIM
    group_size = q_heads // kv_heads
    queries = rotate(
        projected[:, :query_width].reshape(row_len, q_heads, HEAD_DIM), pos_row
    ).astype(jnp.bfloat16)
    queries = queries.reshape(row_len, kv_heads, group_size, HEAD_DIM)
    key_rows = rotate(
        projected[:, query_width : query_width + key_width].reshape(row_len, kv_heads, HEAD_DIM),
        pos_row,
    ).astype(jnp.bfloat16)
    value_rows = (
        projected[:, query_width + key_width :]
        .astype(jnp.bfloat16)
        .reshape(row_len, kv_heads, HEAD_DIM)
    )
    scores = jnp.einsum(
        "rkgd,skd->kgrs", queries, key_rows, preferred_element_type=jnp.float32
    ) * HEAD_DIM ** (-0.5)
    allowed = (id_row[:, None] == id_row[None, :]) & (pos_row[None, :] <= pos_row[:, None])
    allowed = allowed[None, None]
    scores = jnp.where(allowed, scores, -1e30)
    row_top = jnp.max(scores, axis=-1, keepdims=True)
    powers = jnp.where(allowed, jnp.exp(scores - row_top), 0.0)
    weights = (powers / jnp.sum(powers, axis=-1, keepdims=True)).astype(jnp.bfloat16)
    mixed_heads = jnp.einsum(
        "kgrs,skd->rkgd", weights, value_rows, preferred_element_type=jnp.float32
    )
    return mixed_heads.astype(jnp.bfloat16).reshape(row_len, query_width)


def per_device(
    source_tokens, destination, segment_ids, positions, norm_gain, w_query, w_key, w_value, w_out
):
    replicas = lax.axis_size("dp")
    phases = lax.axis_size("section")
    tensors = lax.axis_size("tensor")
    phase_place = lax.axis_index("section")
    tensor_place = lax.axis_index("tensor")
    packed_len = source_tokens.shape[0]
    capacity = packed_len // replicas
    row_count = packed_len // phases
    row_share = row_count // tensors
    matches = destination[:, None] == jnp.arange(replicas, dtype=jnp.int32)[None, :]
    counts = jnp.sum(matches.astype(jnp.int32), axis=0)
    firsts = jnp.min(
        jnp.where(matches, jnp.arange(packed_len, dtype=jnp.int32)[:, None], packed_len), axis=0
    )
    offsets = jnp.arange(capacity, dtype=jnp.int32)
    filled = offsets[None, :] < counts[:, None]
    chosen = jnp.where(filled, firsts[:, None] + offsets[None, :], 0).reshape(-1)
    filled_flat = filled.reshape(-1)
    send_ids = jnp.where(filled_flat, segment_ids[chosen], -1).reshape(replicas, capacity)
    send_pos = jnp.where(filled_flat, positions[chosen], 0).reshape(replicas, capacity)
    send_rows = jnp.where(filled_flat[:, None], source_tokens[chosen], 0).reshape(
        replicas, capacity, -1
    )
    got_rows, got_ids, got_pos = (
        lax.all_to_all(send_rows, "dp", split_axis=0, concat_axis=0, tiled=True),
        lax.all_to_all(send_ids, "dp", split_axis=0, concat_axis=0, tiled=True),
        lax.all_to_all(send_pos, "dp", split_axis=0, concat_axis=0, tiled=True),
    )
    packed = got_rows.reshape(packed_len, -1)
    packed = packed.reshape(phases, row_count, -1)
    id_rows = got_ids.reshape(phases, row_count)
    pos_rows = got_pos.reshape(phases, row_count)
    full_query, full_key, full_value, full_out = (
        lax.all_gather(w_query, "dp", axis=1, tiled=True),
        lax.all_gather(w_key, "dp", axis=1, tiled=True),
        lax.all_gather(w_value, "dp", axis=1, tiled=True),
        lax.all_gather(w_out, "dp", axis=2, tiled=True),
    )
    query_width = full_query.shape[2]
    key_width = full_key.shape[2]
    joined = jnp.concatenate([full_query[0], full_key[0], full_value[0]], axis=1)
    out_rows = full_out[0]
    gain_row = norm_gain[0]
    collected = jnp.zeros((phases, row_share, packed.shape[2]), jnp.bfloat16)
    previous = None
    for moment in range(2 * phases - 1):
        micro_index = jnp.clip(moment - phase_place, 0, phases - 1)
        id_row = lax.dynamic_index_in_dim(id_rows, micro_index, 0, keepdims=False)
        pos_row = lax.dynamic_index_in_dim(pos_rows, micro_index, 0, keepdims=False)
        fresh_rows = packed[moment] if moment < phases else jnp.zeros_like(packed[0])
        if previous is None:
            arriving = jnp.zeros_like(fresh_rows)
        else:
            arriving = shifted(previous, "section", 1)
        current = jnp.where(phase_place == 0, fresh_rows, arriving)
        normed = normalize(current, gain_row)
        projected = jnp.dot(normed, joined, preferred_element_type=jnp.float32)
        mixed_heads = attend_local(projected, id_row, pos_row, query_width, key_width)
        head_terms = jnp.dot(mixed_heads, out_rows, preferred_element_type=jnp.float32)
        head_total = lax.psum(head_terms.astype(jnp.bfloat16), "tensor").astype(jnp.float32)
        result = (current.astype(jnp.float32) + head_total).astype(jnp.bfloat16)
        finished_part = lax.dynamic_slice_in_dim(result, tensor_place * row_share, row_share, 0)
        if moment >= phases - 1:
            collected = collected.at[moment - phases + 1].set(finished_part)
        previous = result
    everything = spread(collected, "section", phases - 1)
    return lax.dynamic_index_in_dim(everything, phase_place, 0, keepdims=False)


def solution(mesh):
    return jax.shard_map(
        per_device,
        mesh=mesh,
        in_specs=(
            P("dp", None),
            P("dp"),
            P("dp"),
            P("dp"),
            P("section", None),
            P("section", "dp", "tensor"),
            P("section", "dp", "tensor"),
            P("section", "dp", "tensor"),
            P("section", "tensor", "dp"),
        ),
        out_specs=P(("dp", "section", "tensor"), None),
        check_vma=False,
    )
```

profile of v0, /device:TPU:0, one launch (start us, length us, event | category | flops | bytes accessed | tf_op | source)
XLA Modules:
  0.0 1037.1 jit_solution(946582375312768616)
XLA Ops:
  9.7 3.5 gather_fusion.1
  13.3 3.5 gather_fusion.2
  17.5 7.3 all-to-all-start.1
  24.9 11.3 %gather_fusion = bf16[512,4096]{1,0:T(8,128)(2,1)} fusion(bf16[512,4096]{1,0:T(8,128)(2,1)} %param.13, s32[1024]{0:T(1024)S(1)} %pad_clamp_fusion), kind=kCustom, calls=%fused_computation | custom fusion | bytes 8390656 | tf_op jit(solution)/shard_map/gather | solution.py:96
  36.2 6.0 all-to-all-start.2
  42.2 4.5 broadcast_select_fusion
  48.7 4.6 all-to-all-start
  58.6 130.9 %all-to-all-done = bf16[8,64,4096]{2,1,0:T(8,128)(2,1)} async-done(((bf16[8,64,4096]{2,1,0:T(8,128)(2,1)}), bf16[8,64,4096]{2,1,0:T(8,128)(2,1)}, u32[]{:S(2)}, u32[]{:S(2)}) %all-to-all-start) | async-done | bytes 4194336 | tf_op jit(solution)/shard_map/all_to_all | solution.py:100
  194.5 37.6 %all-gather.9.cloned.1.call-done = bf16[1,4096,512]{2,1,0:T(8,128)(2,1)} async-done(((bf16[1,512,512]{2,1,0:T(8,128)(2,1)}), bf16[1,4096,512]{2,1,0:T(8,128)(2,1)}) %all-gather.9.cloned.1.call-update) | async-done | bytes 4194320 | tf_op jit(solution)/shard_map/all_gather | solution.py:111
  232.1 228.0 %all-gather.5.cloned.1.call-done = bf16[1,4096,2048]{2,1,0:T(8,128)(2,1)} async-done(((bf16[1,512,2048]{2,1,0:T(8,128)(2,1)}), bf16[1,4096,2048]{2,1,0:T(8,128)(2,1)}) %all-gather.5.cloned.1.call-update) | async-done | bytes 16777232 | tf_op jit(solution)/shard_map/all_gather | solution.py:109
  460.1 14.3 %fusion.102 = f32[256,3072]{1,0:T(8,128)} fusion(bf16[256,4096]{1,0:T(8,128)(2,1)S(1)} %fusion.24, bf16[4096,512]{1,0:T(8,128)(2,1)} %bitcast.200, bf16[4096,512]{1,0:T(8,128)(2,1)} %bitcast.197, bf16[4096,2048]{1,0:T(8,128)(2,1)} %bitcast.194), kind=kOutput, calls=%fused_computation.176 | convolution fusion | flops 6517948416 | bytes 30408704 | tf_op jit(solution)/shard_map/dot_general | solution.py:132
  490.7 3.4 fusion.64
  496.0 192.0 %all-gather.11.cloned.1.call-done = bf16[1,2048,4096]{2,1,0:T(8,128)(2,1)} async-done(((bf16[1,2048,512]{2,1,0:T(8,128)(2,1)}), bf16[1,2048,4096]{2,1,0:T(8,128)(2,1)}) %all-gather.11.cloned.1.call-update) | async-done | bytes 16777232 | tf_op jit(solution)/shard_map/all_gather | solution.py:112
  688.0 11.5 %fusion.9 = bf16[256,4096]{1,0:T(8,128)(2,1)} fusion(bf16[256,2048]{0,1:T(8,128)(2,1)S(1)} %bitcast.175, bf16[1,2048,4096]{2,1,0:T(8,128)(2,1)} %all-gather.11.cloned.1.call-done), kind=kOutput, calls=%fused_computation.16 | convolution fusion | flops 4296015872 | bytes 19922944 | tf_op jit(solution)/shard_map/dot_general | solution.py:134
  699.8 61.0 %all-reduce.5.cloned.1.call-done = bf16[256,4096]{1,0:T(8,128)(2,1)} async-done(((bf16[256,4096]{1,0:T(8,128)(2,1)}), bf16[256,4096]{1,0:T(8,128)(2,1)}) %all-reduce.5.cloned.1.call-update) | async-done | bytes 2097168 | tf_op jit(solution)/shard_map/psum | solution.py:135
  760.8 3.0 fusion.25
  771.7 13.2 %fusion.30 = f32[256,3072]{1,0:T(8,128)} fusion(bf16[256,4096]{1,0:T(8,128)(2,1)S(1)} %get-tuple-element.32, f32[256]{0:T(256)S(1)} %add_rsqrt_fusion.2, f32[4096]{0:T(1024)S(1)} %bitcast.182, bf16[4096,512]{1,0:T(8,128)(2,1)} %bitcast.201, bf16[4096,512]{1,0:T(8,128)(2,1)} %bitcast.198, bf16[4096,2048]{1,0:T(8,128)(2,1)} %bitcast.195), kind=kOutput, calls=%fused_computation.46 | convolution fusion | flops 6522142720 | bytes 30426112 | tf_op jit(solution)/shard_map/dot_general | solution.py:132
  793.7 3.1 slice_negate_fusion.1
  796.8 3.3 copy.96
  800.1 3.1 copy.97
  805.3 4.4 fusion.62
  813.6 5.7 fusion.12
  819.4 63.1 %all-reduce.7.cloned.1.call-done = bf16[256,4096]{1,0:T(8,128)(2,1)} async-done(((bf16[256,4096]{1,0:T(8,128)(2,1)}), bf16[256,4096]{1,0:T(8,128)(2,1)}) %all-reduce.7.cloned.1.call-update) | async-done | bytes 2097168 | tf_op jit(solution)/shard_map/psum | solution.py:135
  887.3 3.0 collective-permute-done.1
  891.7 13.2 %fusion.29 = f32[256,3072]{1,0:T(8,128)} fusion(f32[256]{0:T(256)S(1)} %add_rsqrt_fusion.1, f32[4096]{0:T(1024)S(1)} %bitcast.183, bf16[256,4096]{1,0:T(8,128)(2,1)S(1)} %collective-permute-done.1, pred[]{:T(512)S(6)} %eq.79, bf16[4096,512]{1,0:T(8,128)(2,1)} %bitcast.202, bf16[4096,512]{1,0:T(8,128)(2,1)} %bitcast.199, bf16[4096,2048]{1,0:T(8,128)(2,1)} %bitcast.196), kind=kOutput, calls=%fused_computation.45 | convolution fusion | flops 6523191296 | bytes 30426112 | tf_op jit(solution)/shard_map/dot_general | solution.py:132
  913.7 3.1 slice_negate_fusion
  916.8 3.4 copy.105
  920.1 3.2 copy.106
  925.3 4.4 fusion.60
  933.6 5.8 fusion.15
  943.5 59.0 %all-reduce.9.cloned.1.call-done = bf16[256,4096]{1,0:T(8,128)(2,1)} async-done(((bf16[256,4096]{1,0:T(8,128)(2,1)}), bf16[256,4096]{1,0:T(8,128)(2,1)}) %all-reduce.9.cloned.1.call-update) | async-done | bytes 2097168 | tf_op jit(solution)/shard_map/psum | solution.py:135
  1006.2 21.4 %all-reduce.11.cloned.1.call-done = bf16[2,128,4096]{2,1,0:T(8,128)(2,1)} async-done(((bf16[2,128,4096]{2,1,0:T(8,128)(2,1)}), bf16[2,128,4096]{2,1,0:T(8,128)(2,1)}) %all-reduce.11.cloned.1.call-update) | async-done | bytes 2097168 | tf_op jit(solution)/shard_map/psum | solution.py:21
  (156 shorter events, 87.9 us)
Async XLA Ops:
  6.5 6.7 copy-start.2
  6.5 187.9 %all-gather.7.cloned.1.call-start = ((), (), s32[]{:S(2)}) async-start(), calls=%async_computation.4 | async-start | bytes 4718592 | tf_op jit(solution)/shard_map/all_gather | solution.py:110
  7.3 224.8 %all-gather.9.cloned.1.call-start = ((), (), s32[]{:S(2)}) async-start(), calls=%async_computation.5 | async-start | bytes 4718592 | tf_op jit(solution)/shard_map/all_gather | solution.py:111
  8.0 452.1 %all-gather.5.cloned.1.call-start = ((), (), s32[]{:S(2)}) async-start(), calls=%async_computation.3 | async-start | bytes 18874368 | tf_op jit(solution)/shard_map/all_gather | solution.py:109
  8.7 679.3 %all-gather.11.cloned.1.call-start = ((), (), s32[]{:S(2)}) async-start(), calls=%async_computation.6 | async-start | bytes 18874368 | tf_op jit(solution)/shard_map/all_gather | solution.py:112
  17.5 18.7 %all-to-all-start.1 = ((s32[8,1,64]{2,1,0:T(1,128)}), s32[8,1,64]{2,1,0:T(1,128)S(1)}, u32[]{:S(2)}, u32[]{:S(2)}) async-start(s32[8,1,64]{2,1,0:T(1,128)} %get-tuple-element.61), calls=%async_computation.1 | async-start | bytes 8192 | tf_op jit(solution)/shard_map/all_to_all | solution.py:101
  36.2 12.5 %all-to-all-start.2 = ((s32[8,1,64]{2,1,0:T(1,128)}), s32[8,1,64]{2,1,0:T(1,128)S(1)}, u32[]{:S(2)}, u32[]{:S(2)}) async-start(s32[8,1,64]{2,1,0:T(1,128)} %get-tuple-element.62), calls=%async_computation.2 | async-start | bytes 8192 | tf_op jit(solution)/shard_map/all_to_all | solution.py:102
  46.7 145.1 %copy-start.17 = (f32[1,4096]{1,0:T(1,128)S(1)}, f32[1,4096]{1,0:T(1,128)}, u32[]{:S(2)}) copy-start(f32[1,4096]{1,0:T(1,128)} %param.17) | copy-start | bytes 49156
  48.7 140.8 %all-to-all-start = ((bf16[8,64,4096]{2,1,0:T(8,128)(2,1)}), bf16[8,64,4096]{2,1,0:T(8,128)(2,1)}, u32[]{:S(2)}, u32[]{:S(2)}) async-start(bf16[8,64,4096]{2,1,0:T(8,128)(2,1)} %broadcast_select_fusion), calls=%async_computation | async-start | bytes 8388608 | tf_op jit(solution)/shard_map/all_to_all | solution.py:100
  53.2 707.6 %all-reduce.5.cloned.1.call-start = ((), (), s32[]{:S(2)}) async-start(), calls=%async_computation.7 | async-start | bytes 4194304 | tf_op jit(solution)/shard_map/psum | solution.py:135
  485.9 4.5 copy-start.7
  490.7 3.4 copy-start.15
  699.5 66.2 %copy-start.14 = (f32[256,64]{1,0:T(8,128)S(1)}, f32[256,64]{1,0:T(8,128)}, u32[]{:S(2)}) copy-start(f32[256,64]{1,0:T(8,128)} %get-tuple-element.58) | copy-start | bytes 196612
  699.5 66.3 %copy-start.13 = (f32[256,64]{1,0:T(8,128)S(1)}, f32[256,64]{1,0:T(8,128)}, u32[]{:S(2)}) copy-start(f32[256,64]{1,0:T(8,128)} %get-tuple-element.57) | copy-start | bytes 196612
  699.6 182.9 %all-reduce.7.cloned.1.call-start = ((), (), s32[]{:S(2)}) async-start(), calls=%async_computation.8 | async-start | bytes 4194304 | tf_op jit(solution)/shard_map/psum | solution.py:135
  763.8 5.5 collective-permute-start
  768.4 3.3 copy-start.18
  796.8 8.5 copy-start.8
  805.3 4.5 copy-start.16
  805.3 6.4 slice-start
  805.3 6.4 slice-start.1
  813.6 68.9 %copy-start.6 = (bf16[256,4096]{1,0:T(8,128)(2,1)S(1)}, bf16[256,4096]{1,0:T(8,128)(2,1)}, u32[]{:S(2)}) copy-start(bf16[256,4096]{1,0:T(8,128)(2,1)} %copy-done.5) | copy-start | bytes 6291460
  819.3 67.7 %copy-start.12 = (f32[256,64]{1,0:T(8,128)S(1)}, f32[256,64]{1,0:T(8,128)}, u32[]{:S(2)}) copy-start(f32[256,64]{1,0:T(8,128)} %get-tuple-element.51) | copy-start | bytes 196612
  819.3 72.3 %copy-start.19 = (f32[1,4096]{1,0:T(1,128)S(1)}, f32[1,4096]{1,0:T(1,128)}, u32[]{:S(2)}) copy-start(f32[1,4096]{1,0:T(1,128)} %param.17) | copy-start | bytes 49156
  819.3 183.2 %all-reduce.9.cloned.1.call-start = ((), (), s32[]{:S(2)}) async-start(), calls=%async_computation.9 | async-start | bytes 4194304 | tf_op jit(solution)/shard_map/psum | solution.py:135
  884.8 5.5 copy-start.11
  884.8 5.5 collective-permute-start.1
  916.8 8.6 copy-start.9
  925.3 6.4 slice-start.4
  925.3 6.4 slice-start.5
  939.4 88.1 %all-reduce.11.cloned.1.call-start = ((), (), s32[]{:S(2)}) async-start(), calls=%async_computation.10 | async-start | bytes 4194304 | tf_op jit(solution)/shard_map/psum | solution.py:21
  1002.5 27.3 %copy-start.1 = (s32[512]{0:T(512)S(1)}, s32[512]{0:T(512)}, u32[]{:S(2)}) copy-start(s32[512]{0:T(512)} %param.15) | copy-start | bytes 6148
  (10 other events, 21.8 us)
Sparse Core Ops, SparseCore 0:
  9.5 108.9 all-gather.6
  120.6 111.4 all-gather.8
  234.2 225.8 all-gather.4
  462.0 225.9 all-gather.10
  699.7 61.0 all-reduce.4
  819.5 62.9 all-reduce.6
  939.5 62.9 all-reduce.8
  1006.3 21.1 all-reduce.10
where the time goes:
time: 1040 us
  waiting for transfers between devices  802 us (77%)
  local copies, waits for them, and re-layouts  78.1 us (8%)
  matrix products  77.3 us (7%)
  other arithmetic  43.1 us (4%)
  starting transfers between devices  22.5 us (2%)
  between operations  14.5 us (1%)
    all_gather x1, waiting for transfers between devices, per_device(): lax.all_gather(w_query, 'dp', axis=1, tiled=True)  228 us
    all_gather x1, waiting for transfers between devices, per_device(): lax.all_gather(w_out, 'dp', axis=2, tiled=True)  192 us
    psum x3, waiting for transfers between devices, per_device(): lax.psum(head_terms.astype(jnp.bfloat16), 'tensor').astype(jnp.float32)  183 us
    all_to_all x1, waiting for transfers between devices, per_device(): lax.all_to_all(send_rows, 'dp', split_axis=0, concat_axis=0, tiled=True)  131 us
    dot_general x3, matrix products, per_device(): projected = jnp.dot(normed, joined, preferred_element_type=jnp.float32)  40.7 us
    all_gather x1, waiting for transfers between devices, per_device(): lax.all_gather(w_value, 'dp', axis=1, tiled=True)  37.6 us
    dot_general x3, matrix products, per_device(): jnp.dot(mixed_heads, out_rows, preferred_element_type=jnp.float32)  23 us
    psum x1, waiting for transfers between devices, spread(): return lax.psum(kept, axis)  21.4 us
  transfers between devices with their start and end apart: 13, of which 11 were waited for; matrix products, arithmetic and copies ran while one was open for 7% of the time, Pallas kernels for 0%

commit v1 on v0

v1 whole, which is shorter than its diff:
```python
import jax
import jax.numpy as jnp
from jax import lax
from jax.sharding import PartitionSpec as P

HEAD_DIM = 128


THETA = 500000.0
EPSILON = 1e-05
BF16 = jnp.bfloat16
F32 = jnp.float32


def swapped(array, axis):
    return lax.ppermute(array, axis, [(0, 1), (1, 0)])


def join(array, axis, dim):
    if lax.axis_size(axis) != 2:
        return lax.all_gather(array, axis, axis=dim, tiled=True)
    other = swapped(array, axis)
    first = lax.axis_index(axis) == 0
    return jnp.concatenate(
        [jnp.where(first, array, other), jnp.where(first, other, array)], axis=dim
    )


def sum_share(array, axis):
    if lax.axis_size(axis) != 2:
        return lax.psum_scatter(
            array.astype(BF16), axis, scatter_dimension=0, tiled=True
        ).astype(F32)
    half = array.shape[0] // 2
    first = lax.axis_index(axis) == 0
    mine = jnp.where(first, array[:half], array[half:])
    theirs = jnp.where(first, array[half:], array[:half]).astype(BF16)
    return mine + swapped(theirs, axis).astype(F32)


def both_layers(own, dim, split):
    first = lax.axis_index("section") == 0
    if split:
        half = own.shape[dim] // 2
        low = lax.slice_in_dim(own, 0, half, axis=dim)
        high = lax.slice_in_dim(own, half, 2 * half, axis=dim)
        mine, give = jnp.where(first, low, high), jnp.where(first, high, low)
    else:
        mine = give = own
    got = swapped(give, "section")
    return jnp.where(first, mine, got), jnp.where(first, got, mine)


def ring_order(count):
    return [2 * i for i in range(count // 2)] + [
        2 * i + 1 for i in reversed(range(count // 2))
    ]


def ring_gather(own, before):
    count = lax.axis_size("dp")
    order = ring_order(count)
    right = [(order[i], order[(i + 1) % count]) for i in range(count)]
    left = [(b, a) for a, b in right]
    parts = [None] * count
    parts[0] = own
    onward = back = own
    if before is not None:
        onward, back, _, _ = lax.optimization_barrier((own, own) + before)
    for hop in range(1, count // 2):
        onward = lax.ppermute(onward, "dp", right)
        back = lax.ppermute(back, "dp", left)
        parts[hop], parts[count - hop] = onward, back
    half = own.shape[0] // 2
    top = lax.ppermute(onward[:half], "dp", right)
    low = lax.ppermute(back[half:], "dp", left)
    parts[count // 2] = jnp.concatenate([top, low], axis=0)
    return parts, (onward, back)


def turn_factors(places):
    half_dim = HEAD_DIM // 2
    frequency = THETA ** (-(jnp.arange(half_dim, dtype=F32) * 2.0) / HEAD_DIM)
    angles = places.astype(F32)[..., None] * frequency
    cosine, sine = jnp.cos(angles), jnp.sin(angles)
    return (
        jnp.concatenate([cosine, cosine], axis=-1)[..., None, :],
        jnp.concatenate([sine, sine], axis=-1)[..., None, :],
    )


def rotate(values, factors):
    half_dim = HEAD_DIM // 2
    turned = jnp.concatenate([-values[..., half_dim:], values[..., :half_dim]], axis=-1)
    return values * factors[0] + turned * factors[1]


def attend_local(projected, allowed, factors, query_width, key_width):
    batches, row_len = allowed.shape[:2]
    q_heads = query_width // HEAD_DIM
    kv_heads = key_width // HEAD_DIM
    group_size = q_heads // kv_heads
    projected = projected.reshape(batches, row_len, -1)
    queries = rotate(
        projected[..., :query_width].reshape(batches, row_len, q_heads, HEAD_DIM), factors
    ).astype(BF16)
    queries = queries.reshape(batches, row_len, kv_heads, group_size, HEAD_DIM)
    key_rows = rotate(
        projected[..., query_width : query_width + key_width].reshape(
            batches, row_len, kv_heads, HEAD_DIM
        ),
        factors,
    ).astype(BF16)
    value_rows = (
        projected[..., query_width + key_width :]
        .astype(BF16)
        .reshape(batches, row_len, kv_heads, HEAD_DIM)
    )
    scores = jnp.einsum(
        "brkgd,bskd->bkgrs", queries, key_rows, preferred_element_type=F32
    ) * HEAD_DIM ** (-0.5)
    allowed = allowed[:, None, None]
    scores = jnp.where(allowed, scores, -1e30)
    row_top = jnp.max(scores, axis=-1, keepdims=True)
    powers = jnp.where(allowed, jnp.exp(scores - row_top), 0.0)
    weights = (powers / jnp.sum(powers, axis=-1, keepdims=True)).astype(BF16)
    mixed_heads = jnp.einsum(
        "bkgrs,bskd->brkgd", weights, value_rows, preferred_element_type=F32
    )
    return mixed_heads.astype(BF16).reshape(batches * row_len, query_width)


def per_device(
    source_tokens, destination, segment_ids, positions, norm_gain, w_query, w_key, w_value, w_out
):
    replicas = lax.axis_size("dp")
    phases = lax.axis_size("section")
    tensors = lax.axis_size("tensor")
    section = lax.axis_index("section")
    tensor = lax.axis_index("tensor")
    packed_len, width = source_tokens.shape
    capacity = packed_len // replicas
    row_count = packed_len // phases
    row_share = row_count // tensors
    chunk = width // replicas
    place = lax.axis_index("dp")
    spot = jnp.where(place % 2 == 0, place // 2, replicas - 1 - place // 2)

    def start_of(k):
        there = (spot - k + replicas) % replicas
        owner = jnp.where(there < replicas // 2, 2 * there, 2 * (replicas - 1 - there) + 1)
        return owner * chunk

    split = (w_key.shape[2] // HEAD_DIM) % phases == 0
    query_parts = both_layers(w_query[0], 1, True)
    kv_parts = both_layers(
        jnp.stack([w_key[0], w_value[0]], axis=1), 2, split
    )
    query_width = query_parts[0].shape[1]
    key_width = kv_parts[0].shape[2]
    joined = [
        jnp.concatenate([q, kv.reshape(kv.shape[0], -1)], axis=1)
        for q, kv in zip(query_parts, kv_parts)
    ]
    out_parts = both_layers(w_out[0], 0, True)
    first = section == 0
    other_gain = swapped(norm_gain[0], "section")
    gains = (
        jnp.where(first, norm_gain[0], other_gain),
        jnp.where(first, other_gain, norm_gain[0]),
    )

    matches = destination[:, None] == jnp.arange(replicas, dtype=jnp.int32)[None, :]
    counts = jnp.sum(matches.astype(jnp.int32), axis=0)
    firsts = jnp.min(
        jnp.where(matches, jnp.arange(packed_len, dtype=jnp.int32)[:, None], packed_len), axis=0
    )
    offsets = jnp.arange(capacity, dtype=jnp.int32)
    filled = offsets[None, :] < counts[:, None]
    chosen = jnp.where(filled, firsts[:, None] + offsets[None, :], 0).reshape(-1)
    filled_flat = filled.reshape(-1)
    share = width // (phases * tensors)
    columns = lax.dynamic_slice_in_dim(
        source_tokens, (section * tensors + tensor) * share, share, 1
    )
    send_rows = jnp.where(filled_flat[:, None], columns[chosen], 0).reshape(
        replicas, capacity, share
    )
    send_ids = jnp.where(filled_flat, segment_ids[chosen], -1).reshape(replicas, capacity)
    send_pos = jnp.where(filled_flat, positions[chosen], 0).reshape(replicas, capacity)
    got_rows = lax.all_to_all(send_rows, "dp", split_axis=0, concat_axis=0, tiled=True)
    got_marks = lax.all_to_all(
        jnp.concatenate([send_ids, send_pos], axis=1), "dp", split_axis=0, concat_axis=0, tiled=True
    )
    packed = join(join(got_rows.reshape(packed_len, share), "tensor", 1), "section", 1)
    id_rows = got_marks[:, :capacity].reshape(phases, row_count)
    pos_rows = got_marks[:, capacity:].reshape(phases, row_count)
    factors = turn_factors(pos_rows)
    allowed = (id_rows[:, :, None] == id_rows[:, None, :]) & (
        pos_rows[:, None, :] <= pos_rows[:, :, None]
    )

    starts = [start_of(k) for k in range(replicas)]
    states = [lax.dynamic_slice_in_dim(packed, s, chunk, 1) for s in starts]
    before = None
    for level in range(phases):
        projections, before = ring_gather(joined[level], before)
        outs, before = ring_gather(out_parts[level], before)
        total = sum(
            jnp.sum(jnp.square(piece.astype(F32)), axis=-1, keepdims=True) for piece in states
        )
        inv_scale = lax.rsqrt(total / width + EPSILON)
        projected = 0.0
        for k in range(replicas):
            gain = lax.dynamic_slice_in_dim(gains[level], starts[k], chunk, 0)
            normed = (states[k].astype(F32) * inv_scale * gain).astype(BF16)
            projected += jnp.dot(normed, projections[k], preferred_element_type=F32)
        mixed_heads = attend_local(projected, allowed, factors, query_width, key_width)
        fresh = [None] * replicas
        half = replicas // 2
        rounds = [[0]] + [[k, replicas - k] for k in range(1, half)] + [[half]]
        for members in rounds:
            terms = jnp.concatenate(
                [jnp.dot(mixed_heads, outs[k], preferred_element_type=F32) for k in members],
                axis=1,
            )
            share_sum = sum_share(sum_share(terms, "section"), "tensor")
            held = jnp.concatenate([states[k] for k in members], axis=1)
            held = lax.dynamic_slice_in_dim(
                held, section * row_count + tensor * row_share, row_share, 0
            )
            result = (held.astype(F32) + share_sum).astype(BF16)
            if level < phases - 1:
                result = join(join(result, "tensor", 0), "section", 0)
            for i, k in enumerate(members):
                fresh[k] = lax.slice_in_dim(result, i * chunk, (i + 1) * chunk, axis=1)
        states = fresh
    final = jnp.zeros((row_share, width), BF16)
    for k in range(replicas):
        final = lax.dynamic_update_slice_in_dim(final, states[k], starts[k], 1)
    return final


def solution(mesh):
    return jax.shard_map(
        per_device,
        mesh=mesh,
        in_specs=(
            P("dp", None),
            P("dp"),
            P("dp"),
            P("dp"),
            P("section", None),
            P("section", "dp", "tensor"),
            P("section", "dp", "tensor"),
            P("section", "dp", "tensor"),
            P("section", "tensor", "dp"),
        ),
        out_specs=P(("dp", "section", "tensor"), None),
        check_vma=False,
    )
```

time: 1040 us -> 529 us (0.51)
  waiting for transfers between devices: 802 us -> 302 us
  starting transfers between devices: 22.5 us -> 68.2 us
  local copies, waits for them, and re-layouts: 78.1 us -> 45.7 us
  matrix products: 77.3 us -> 55.2 us
  between operations: 14.5 us -> 2.17 us
    all_gather x4 -> x0, waiting for transfers between devices: 458 us -> none  [the longest x1 228 us: per_device(): lax.all_gather(w_query, 'dp', axis=1, tiled=True)]
    ppermute x2 -> x68, waiting for transfers between devices: 3.9 us -> 283 us  [the longest x12 128 us: ring_gather(): onward = lax.ppermute(onward, 'dp', right)]
    psum x4 -> x0, waiting for transfers between devices: 204 us -> none  [the longest x3 183 us: per_device(): lax.psum(head_terms.astype(jnp.bfloat16), 'tensor').astype(jnp.float32)]
    all_to_all x1, waiting for transfers between devices: 131 us -> 19.8 us  [per_device(): lax.all_to_all(send_rows, 'dp', split_axis=0, concat_axis=0, tiled=True)]
    ppermute x2 -> x68, starting transfers between devices: 4 us -> 55.6 us  [the longest x36 20.5 us: swapped(): return lax.ppermute(array, axis, [(0, 1), (1, 0)])]
    dot_general x12 -> x36, matrix products: 77.3 us -> 55.2 us  [the longest x16 23.6 us: per_device(): projected += jnp.dot(normed, projections[k], preferred_element_type=F32)]
    concatenate x6 -> x0, local copies, waits for them, and re-layouts: 16.7 us -> none  [rotate(): jnp.concatenate([-values[..., half_dim:], values[..., :half_dim]], axis=-1)]
    select_n x3 -> x21, other arithmetic: 6.05 us -> 16.8 us  [the longest x3 6.04 us: both_layers(): return (jnp.where(first, mine, got), jnp.where(first, got, mine))]
  transfers between devices with their start and end apart: 13 -> 70, of which waited for: 11 -> 33; matrix products, arithmetic and copies ran while one was open for 7% -> 26% of each run, Pallas kernels for 0% -> 0%
where the time goes in v1:
time: 529 us; the launch traced here: 520 us
  waiting for transfers between devices  302 us (57%)
  starting transfers between devices  68.2 us (13%)
  matrix products  55.2 us (10%)
  other arithmetic  46.2 us (9%)
  local copies, waits for them, and re-layouts  45.7 us (9%)
    ppermute x12, waiting for transfers between devices, ring_gather(): onward = lax.ppermute(onward, 'dp', right)  128 us
    ppermute x36, waiting for transfers between devices, swapped(): return lax.ppermute(array, axis, [(0, 1), (1, 0)])  59.1 us
    ppermute x12, waiting for transfers between devices, ring_gather(): back = lax.ppermute(back, 'dp', left)  48.5 us
    ppermute x4, waiting for transfers between devices, ring_gather(): top = lax.ppermute(onward[:half], 'dp', right)  31.7 us
    dot_general x16, matrix products, per_device(): projected += jnp.dot(normed, projections[k], preferred_element_type=F32)  23.6 us
    ppermute x36, starting transfers between devices, swapped(): return lax.ppermute(array, axis, [(0, 1), (1, 0)])  20.5 us
    all_to_all x1, waiting for transfers between devices, per_device(): lax.all_to_all(send_rows, 'dp', split_axis=0, concat_axis=0, tiled=True)  19.8 us
    dot_general x16, matrix products, per_device(): jnp.dot(mixed_heads, outs[k], preferred_element_type=F32)  19.2 us
  transfers between devices with their start and end apart: 70, of which 33 were waited for; matrix products, arithmetic and copies ran while one was open for 26% of the time, Pallas kernels for 0%

profile of v1, /device:TPU:0, one launch (start us, length us, event | category | flops | bytes accessed | tf_op | source)
XLA Modules:
  0.0 519.9 jit_solution(10391708088268549370)
XLA Ops:
  7.7 7.4 %all-to-all-start = ((bf16[8,64,1024]{2,1,0:T(8,128)(2,1)}), bf16[8,64,1024]{2,1,0:T(8,128)(2,1)}, u32[]{:S(2)}, u32[]{:S(2)}) async-start(bf16[8,64,1024]{2,1,0:T(8,128)(2,1)} %broadcast_select_fusion.7), calls=%async_computation | async-start | bytes 2097152 | tf_op jit(solution)/shard_map/all_to_all | solution.py:191
  21.2 19.8 %all-to-all-done = bf16[8,64,1024]{2,1,0:T(8,128)(2,1)} async-done(((bf16[8,64,1024]{2,1,0:T(8,128)(2,1)}), bf16[8,64,1024]{2,1,0:T(8,128)(2,1)}, u32[]{:S(2)}, u32[]{:S(2)}) %all-to-all-start) | async-done | bytes 1048608 | tf_op jit(solution)/shard_map/all_to_all | solution.py:191
  48.0 3.5 gather_fusion.1
  51.5 3.5 gather_fusion.2
  55.2 9.5 %collective-permute-done = bf16[512,1024]{1,0:T(8,128)(2,1)} collective-permute-done((bf16[512,1024]{1,0:T(8,128)(2,1)}, bf16[512,1024]{1,0:T(8,128)(2,1)}, u32[]{:S(2)}, u32[]{:S(2)}) %collective-permute-start) | collective-permute-done | bytes 1048608 | tf_op jit(solution)/shard_map/ppermute | solution.py:16
  69.5 5.2 %all-to-all-start.1 = ((s32[8,1,128]{2,1,0:T(1,128)}), s32[8,1,128]{2,1,0:T(1,128)S(1)}, u32[]{:S(2)}, u32[]{:S(2)}) async-start(s32[8,1,128]{2,1,0:T(1,128)} %bitcast.12), calls=%async_computation.1 | async-start | bytes 8192 | tf_op jit(solution)/shard_map/all_to_all | solution.py:192
  76.1 4.9 collective-permute-done.5
  92.0 24.3 %collective-permute-done.10 = bf16[512,1536]{1,0:T(8,128)(2,1)} collective-permute-done((bf16[512,1536]{1,0:T(8,128)(2,1)}, bf16[512,1536]{1,0:T(8,128)(2,1)}, u32[]{:S(2)}, u32[]{:S(2)}) %collective-permute-start.10) | collective-permute-done | bytes 1572896 | tf_op jit(solution)/shard_map/ppermute | solution.py:72
  123.2 3.1 fusion.132
  130.2 20.5 %collective-permute-done.11 = bf16[512,1536]{1,0:T(8,128)(2,1)S(1)} collective-permute-done((bf16[512,1536]{1,0:T(8,128)(2,1)}, bf16[512,1536]{1,0:T(8,128)(2,1)S(1)}, u32[]{:S(2)}, u32[]{:S(2)}) %collective-permute-start.11) | collective-permute-done | bytes 1572896 | tf_op jit(solution)/shard_map/ppermute | solution.py:72
  160.4 11.3 %collective-permute-done.12 = bf16[256,1536]{1,0:T(8,128)(2,1)S(1)} collective-permute-done((bf16[256,1536]{1,0:T(8,128)(2,1)S(1)}, bf16[256,1536]{1,0:T(8,128)(2,1)S(1)}, u32[]{:S(2)}, u32[]{:S(2)}) %collective-permute-start.12) | collective-permute-done | bytes 786464 | tf_op jit(solution)/shard_map/ppermute | solution.py:76
  187.7 3.4 fusion.90
  191.1 4.0 fusion.227
  198.6 3.6 fusion.32
  217.6 7.2 %collective-permute-done.21 = bf16[128,1024]{1,0:T(8,128)(2,1)S(1)} collective-permute-done((bf16[128,1024]{1,0:T(8,128)(2,1)S(1)}, bf16[128,1024]{1,0:T(8,128)(2,1)S(1)}, u32[]{:S(2)}, u32[]{:S(2)}) %collective-permute-start.21) | collective-permute-done | bytes 262176 | tf_op jit(solution)/shard_map/ppermute | solution.py:16
  225.6 14.3 %collective-permute-done.24 = bf16[1024,512]{1,0:T(8,128)(2,1)S(1)} collective-permute-done((bf16[1024,512]{1,0:T(8,128)(2,1)}, bf16[1024,512]{1,0:T(8,128)(2,1)S(1)}, u32[]{:S(2)}, u32[]{:S(2)}) %collective-permute-start.24) | collective-permute-done | bytes 1048608 | tf_op jit(solution)/shard_map/ppermute | solution.py:71
  248.1 6.0 %collective-permute-done.27 = bf16[128,1024]{1,0:T(8,128)(2,1)S(1)} collective-permute-done((bf16[128,1024]{1,0:T(8,128)(2,1)S(1)}, bf16[128,1024]{1,0:T(8,128)(2,1)S(1)}, u32[]{:S(2)}, u32[]{:S(2)}) %collective-permute-start.27) | collective-permute-done | bytes 262176 | tf_op jit(solution)/shard_map/ppermute | solution.py:16
  255.1 13.3 %collective-permute-done.30 = bf16[1024,512]{1,0:T(8,128)(2,1)S(1)} collective-permute-done((bf16[1024,512]{1,0:T(8,128)(2,1)S(1)}, bf16[1024,512]{1,0:T(8,128)(2,1)S(1)}, u32[]{:S(2)}, u32[]{:S(2)}) %collective-permute-start.30) | collective-permute-done | bytes 1048608 | tf_op jit(solution)/shard_map/ppermute | solution.py:71
  274.1 9.2 %collective-permute-done.36 = bf16[512,512]{1,0:T(8,128)(2,1)S(1)} collective-permute-done((bf16[512,512]{1,0:T(8,128)(2,1)S(1)}, bf16[512,512]{1,0:T(8,128)(2,1)S(1)}, u32[]{:S(2)}, u32[]{:S(2)}) %collective-permute-start.36) | collective-permute-done | bytes 524320 | tf_op jit(solution)/shard_map/ppermute | solution.py:75
  289.9 8.5 %collective-permute-done.39 = bf16[128,512]{1,0:T(8,128)(2,1)S(1)} collective-permute-done((bf16[128,512]{1,0:T(8,128)(2,1)S(1)}, bf16[128,512]{1,0:T(8,128)(2,1)S(1)}, u32[]{:S(2)}, u32[]{:S(2)}) %collective-permute-start.39) | collective-permute-done | bytes 131104 | tf_op jit(solution)/shard_map/ppermute | solution.py:16
  300.5 14.4 %collective-permute-done.42 = bf16[512,1536]{1,0:T(8,128)(2,1)S(1)} collective-permute-done((bf16[512,1536]{1,0:T(8,128)(2,1)S(1)}, bf16[512,1536]{1,0:T(8,128)(2,1)S(1)}, u32[]{:S(2)}, u32[]{:S(2)}) %collective-permute-start.42) | collective-permute-done | bytes 1572896 | tf_op jit(solution)/shard_map/ppermute | solution.py:71
  319.3 6.2 %collective-permute-done.40 = bf16[128,512]{1,0:T(8,128)(2,1)S(1)} collective-permute-done((bf16[128,512]{1,0:T(8,128)(2,1)S(1)}, bf16[128,512]{1,0:T(8,128)(2,1)S(1)}, u32[]{:S(2)}, u32[]{:S(2)}) %collective-permute-start.40) | collective-permute-done | bytes 131104 | tf_op jit(solution)/shard_map/ppermute | solution.py:16
  326.6 22.8 %collective-permute-done.43 = bf16[512,1536]{1,0:T(8,128)(2,1)S(1)} collective-permute-done((bf16[512,1536]{1,0:T(8,128)(2,1)S(1)}, bf16[512,1536]{1,0:T(8,128)(2,1)S(1)}, u32[]{:S(2)}, u32[]{:S(2)}) %collective-permute-start.43) | collective-permute-done | bytes 1572896 | tf_op jit(solution)/shard_map/ppermute | solution.py:71
  354.6 29.2 %collective-permute-done.44 = bf16[512,1536]{1,0:T(8,128)(2,1)S(1)} collective-permute-done((bf16[512,1536]{1,0:T(8,128)(2,1)S(1)}, bf16[512,1536]{1,0:T(8,128)(2,1)S(1)}, u32[]{:S(2)}, u32[]{:S(2)}) %collective-permute-start.44) | collective-permute-done | bytes 1572896 | tf_op jit(solution)/shard_map/ppermute | solution.py:71
  391.6 12.8 %collective-permute-done.45 = bf16[256,1536]{1,0:T(8,128)(2,1)S(1)} collective-permute-done((bf16[256,1536]{1,0:T(8,128)(2,1)S(1)}, bf16[256,1536]{1,0:T(8,128)(2,1)S(1)}, u32[]{:S(2)}, u32[]{:S(2)}) %collective-permute-start.45) | collective-permute-done | bytes 786464 | tf_op jit(solution)/shard_map/ppermute | solution.py:75
  422.4 3.4 fusion.228
  440.6 17.4 %collective-permute-done.56 = bf16[1024,512]{1,0:T(8,128)(2,1)S(1)} collective-permute-done((bf16[1024,512]{1,0:T(8,128)(2,1)}, bf16[1024,512]{1,0:T(8,128)(2,1)S(1)}, u32[]{:S(2)}, u32[]{:S(2)}) %collective-permute-start.56) | collective-permute-done | bytes 1048608 | tf_op jit(solution)/shard_map/ppermute | solution.py:71
  467.7 4.7 collective-permute-done.55
  472.6 4.9 collective-permute-done.59
  477.8 12.2 %collective-permute-done.60 = bf16[1024,512]{1,0:T(8,128)(2,1)S(1)} collective-permute-done((bf16[1024,512]{1,0:T(8,128)(2,1)S(1)}, bf16[1024,512]{1,0:T(8,128)(2,1)S(1)}, u32[]{:S(2)}, u32[]{:S(2)}) %collective-permute-start.60) | collective-permute-done | bytes 1048608 | tf_op jit(solution)/shard_map/ppermute | solution.py:71
  493.9 9.4 %collective-permute-done.64 = bf16[512,512]{1,0:T(8,128)(2,1)S(1)} collective-permute-done((bf16[512,512]{1,0:T(8,128)(2,1)S(1)}, bf16[512,512]{1,0:T(8,128)(2,1)S(1)}, u32[]{:S(2)}, u32[]{:S(2)}) %collective-permute-start.64) | collective-permute-done | bytes 524320 | tf_op jit(solution)/shard_map/ppermute | solution.py:75
  508.4 6.8 %collective-permute-done.63 = bf16[128,1024]{1,0:T(8,128)(2,1)S(1)} collective-permute-done((bf16[128,1024]{1,0:T(8,128)(2,1)S(1)}, bf16[128,1024]{1,0:T(8,128)(2,1)S(1)}, u32[]{:S(2)}, u32[]{:S(2)}) %collective-permute-start.63) | collective-permute-done | bytes 262176 | tf_op jit(solution)/shard_map/ppermute | solution.py:16
  (413 shorter events, 191.0 us)
Async XLA Ops:
  7.7 33.3 %all-to-all-start = ((bf16[8,64,1024]{2,1,0:T(8,128)(2,1)}), bf16[8,64,1024]{2,1,0:T(8,128)(2,1)}, u32[]{:S(2)}, u32[]{:S(2)}) async-start(bf16[8,64,1024]{2,1,0:T(8,128)(2,1)} %broadcast_select_fusion.7), calls=%async_computation | async-start | bytes 2097152 | tf_op jit(solution)/shard_map/all_to_all | solution.py:191
  16.1 26.3 %collective-permute-start.3 = (bf16[512,1024]{1,0:T(8,128)(2,1)}, bf16[512,1024]{1,0:T(8,128)(2,1)}, u32[]{:S(2)}, u32[]{:S(2)}) collective-permute-start(bf16[512,1024]{1,0:T(8,128)(2,1)} %broadcast_select_fusion.5), channel_id=1, source_target_pairs={{0,2},{2,0},{1,3},{3,1},{4,6},{6,4},{5,7},{7,5},{8,10},{10,8},{9,1... | collective-permute-start | bytes 3145736 | tf_op jit(solution)/shard_map/ppermute | solution.py:16
  45.9 35.1 %collective-permute-start.5 = (bf16[512,1536]{1,0:T(8,128)(2,1)}, bf16[512,1536]{1,0:T(8,128)(2,1)}, u32[]{:S(2)}, u32[]{:S(2)}) collective-permute-start(bf16[512,1536]{1,0:T(8,128)(2,1)} %pad_maximum_fusion.1), channel_id=1, source_target_pairs={{0,8},{8,16},{16,24},{24,28},{28,20},{20,12},{12,4},{4,0},{1,9},{9... | collective-permute-start | bytes 4718600 | tf_op jit(solution)/shard_map/ppermute | solution.py:71
  45.9 35.1 %collective-permute-start.9 = (bf16[512,1536]{1,0:T(8,128)(2,1)}, bf16[512,1536]{1,0:T(8,128)(2,1)}, u32[]{:S(2)}, u32[]{:S(2)}) collective-permute-start(bf16[512,1536]{1,0:T(8,128)(2,1)} %pad_maximum_fusion.1), channel_id=1, source_target_pairs={{8,0},{16,8},{24,16},{28,24},{20,28},{12,20},{4,12},{0,4},{9,1},{1... | collective-permute-start | bytes 4718600 | tf_op jit(solution)/shard_map/ppermute | solution.py:72
  47.9 36.9 %collective-permute-start.2 = (f32[4096]{0:T(1024)}, f32[4096]{0:T(1024)}, u32[]{:S(2)}, u32[]{:S(2)}) collective-permute-start(f32[4096]{0:T(1024)} %bitcast.3), channel_id=1, source_target_pairs={{0,2},{2,0},{1,3},{3,1},{4,6},{6,4},{5,7},{7,5},{8,10},{10,8},{9,1... | collective-permute-start | bytes 49160 | tf_op jit(solution)/shard_map/ppermute | solution.py:16
  68.9 49.4 %collective-permute-start.1 = (bf16[512,2048]{1,0:T(8,128)(2,1)}, bf16[512,2048]{1,0:T(8,128)(2,1)}, u32[]{:S(2)}, u32[]{:S(2)}) collective-permute-start(bf16[512,2048]{1,0:T(8,128)(2,1)} %pad_maximum_fusion), channel_id=1, source_target_pairs={{0,2},{2,0},{1,3},{3,1},{4,6},{6,4},{5,7},{7,5},{8,10},{10,8},{9,1... | collective-permute-start | bytes 6291464 | tf_op jit(solution)/shard_map/ppermute | solution.py:16
  81.0 36.2 %collective-permute-start.6 = (bf16[512,1536]{1,0:T(8,128)(2,1)}, bf16[512,1536]{1,0:T(8,128)(2,1)}, u32[]{:S(2)}, u32[]{:S(2)}) collective-permute-start(bf16[512,1536]{1,0:T(8,128)(2,1)} %collective-permute-done.5), channel_id=1, source_target_pairs={{0,8},{8,16},{16,24},{24,28},{28,20},{20,12},{12,4},{4,0},{1,9},{9... | collective-permute-start | bytes 4718600 | tf_op jit(solution)/shard_map/ppermute | solution.py:71
  81.0 35.3 %collective-permute-start.10 = (bf16[512,1536]{1,0:T(8,128)(2,1)}, bf16[512,1536]{1,0:T(8,128)(2,1)}, u32[]{:S(2)}, u32[]{:S(2)}) collective-permute-start(bf16[512,1536]{1,0:T(8,128)(2,1)} %collective-permute-done.9), channel_id=1, source_target_pairs={{8,0},{16,8},{24,16},{28,24},{20,28},{12,20},{4,12},{0,4},{9,1},{1... | collective-permute-start | bytes 4718600 | tf_op jit(solution)/shard_map/ppermute | solution.py:72
  116.3 34.4 %collective-permute-start.11 = (bf16[512,1536]{1,0:T(8,128)(2,1)}, bf16[512,1536]{1,0:T(8,128)(2,1)S(1)}, u32[]{:S(2)}, u32[]{:S(2)}) collective-permute-start(bf16[512,1536]{1,0:T(8,128)(2,1)} %collective-permute-done.10), channel_id=1, source_target_pairs={{8,0},{16,8},{24,16},{28,24},{20,28},{12,20},{4,12},{0,4},{9,1},{1... | collective-permute-start | bytes 4718600 | tf_op jit(solution)/shard_map/ppermute | solution.py:72
  117.2 34.2 %collective-permute-start.7 = (bf16[512,1536]{1,0:T(8,128)(2,1)}, bf16[512,1536]{1,0:T(8,128)(2,1)S(1)}, u32[]{:S(2)}, u32[]{:S(2)}) collective-permute-start(bf16[512,1536]{1,0:T(8,128)(2,1)} %collective-permute-done.6), channel_id=1, source_target_pairs={{0,8},{8,16},{16,24},{24,28},{28,20},{20,12},{12,4},{4,0},{1,9},{9... | collective-permute-start | bytes 4718600 | tf_op jit(solution)/shard_map/ppermute | solution.py:71
  158.3 48.9 %collective-permute-start.18 = (bf16[1024,512]{1,0:T(8,128)(2,1)}, bf16[1024,512]{1,0:T(8,128)(2,1)}, u32[]{:S(2)}, u32[]{:S(2)}) collective-permute-start(bf16[1024,512]{1,0:T(8,128)(2,1)} %get-tuple-element.12), channel_id=1, source_target_pairs={{0,8},{8,16},{16,24},{24,28},{28,20},{20,12},{12,4},{4,0},{1,9},{9... | collective-permute-start | bytes 3145736 | tf_op jit(solution)/shard_map/ppermute | solution.py:71
  160.1 49.4 %collective-permute-start.19 = (bf16[1024,512]{1,0:T(8,128)(2,1)}, bf16[1024,512]{1,0:T(8,128)(2,1)}, u32[]{:S(2)}, u32[]{:S(2)}) collective-permute-start(bf16[1024,512]{1,0:T(8,128)(2,1)} %get-tuple-element.12), channel_id=1, source_target_pairs={{8,0},{16,8},{24,16},{28,24},{20,28},{12,20},{4,12},{0,4},{9,1},{1... | collective-permute-start | bytes 3145736 | tf_op jit(solution)/shard_map/ppermute | solution.py:72
  214.3 25.5 %collective-permute-start.24 = (bf16[1024,512]{1,0:T(8,128)(2,1)}, bf16[1024,512]{1,0:T(8,128)(2,1)S(1)}, u32[]{:S(2)}, u32[]{:S(2)}) collective-permute-start(bf16[1024,512]{1,0:T(8,128)(2,1)} %collective-permute-done.18), channel_id=1, source_target_pairs={{0,8},{8,16},{16,24},{24,28},{28,20},{20,12},{12,4},{4,0},{1,9},{9... | collective-permute-start | bytes 3145736 | tf_op jit(solution)/shard_map/ppermute | solution.py:71
  216.1 25.2 %collective-permute-start.25 = (bf16[1024,512]{1,0:T(8,128)(2,1)}, bf16[1024,512]{1,0:T(8,128)(2,1)S(1)}, u32[]{:S(2)}, u32[]{:S(2)}) collective-permute-start(bf16[1024,512]{1,0:T(8,128)(2,1)} %collective-permute-done.19), channel_id=1, source_target_pairs={{8,0},{16,8},{24,16},{28,24},{20,28},{12,20},{4,12},{0,4},{9,1},{1... | collective-permute-start | bytes 3145736 | tf_op jit(solution)/shard_map/ppermute | solution.py:72
  243.0 46.9 %collective-permute-start.15 = (bf16[128,512]{1,0:T(8,128)(2,1)S(1)}, bf16[128,512]{1,0:T(8,128)(2,1)S(1)}, u32[]{:S(2)}, u32[]{:S(2)}) collective-permute-start(bf16[128,512]{1,0:T(8,128)(2,1)S(1)} %select_convert_fusion.19), channel_id=1, source_target_pairs={{0,1},{1,0},{2,3},{3,2},{4,5},{5,4},{6,7},{7,6},{8,9},{9,8},{10,11... | collective-permute-start | bytes 393224 | tf_op jit(solution)/shard_map/ppermute | solution.py:16
  243.6 24.8 %collective-permute-start.30 = (bf16[1024,512]{1,0:T(8,128)(2,1)S(1)}, bf16[1024,512]{1,0:T(8,128)(2,1)S(1)}, u32[]{:S(2)}, u32[]{:S(2)}) collective-permute-start(bf16[1024,512]{1,0:T(8,128)(2,1)S(1)} %collective-permute-done.24), channel_id=1, source_target_pairs={{0,8},{8,16},{16,24},{24,28},{28,20},{20,12},{12,4},{4,0},{1,9},{9... | collective-permute-start | bytes 3145736 | tf_op jit(solution)/shard_map/ppermute | solution.py:71
  245.3 24.9 %collective-permute-start.31 = (bf16[1024,512]{1,0:T(8,128)(2,1)S(1)}, bf16[1024,512]{1,0:T(8,128)(2,1)S(1)}, u32[]{:S(2)}, u32[]{:S(2)}) collective-permute-start(bf16[1024,512]{1,0:T(8,128)(2,1)S(1)} %collective-permute-done.25), channel_id=1, source_target_pairs={{8,0},{16,8},{24,16},{28,24},{20,28},{12,20},{4,12},{0,4},{9,1},{1... | collective-permute-start | bytes 3145736 | tf_op jit(solution)/shard_map/ppermute | solution.py:72
  272.2 42.6 %collective-permute-start.42 = (bf16[512,1536]{1,0:T(8,128)(2,1)S(1)}, bf16[512,1536]{1,0:T(8,128)(2,1)S(1)}, u32[]{:S(2)}, u32[]{:S(2)}) collective-permute-start(bf16[512,1536]{1,0:T(8,128)(2,1)S(1)} %pad_maximum_fusion.2), channel_id=1, source_target_pairs={{0,8},{8,16},{16,24},{24,28},{28,20},{20,12},{12,4},{4,0},{1,9},{9... | collective-permute-start | bytes 4718600 | tf_op jit(solution)/shard_map/ppermute | solution.py:71
  283.3 33.3 %collective-permute-start.46 = (bf16[512,1536]{1,0:T(8,128)(2,1)S(1)}, bf16[512,1536]{1,0:T(8,128)(2,1)S(1)}, u32[]{:S(2)}, u32[]{:S(2)}) collective-permute-start(bf16[512,1536]{1,0:T(8,128)(2,1)S(1)} %pad_maximum_fusion.2), channel_id=1, source_target_pairs={{8,0},{16,8},{24,16},{28,24},{20,28},{12,20},{4,12},{0,4},{9,1},{1... | collective-permute-start | bytes 4718600 | tf_op jit(solution)/shard_map/ppermute | solution.py:72
  287.1 29.8 %collective-permute-start.33 = (bf16[128,1024]{1,0:T(8,128)(2,1)S(1)}, bf16[128,1024]{1,0:T(8,128)(2,1)S(1)}, u32[]{:S(2)}, u32[]{:S(2)}) collective-permute-start(bf16[128,1024]{1,0:T(8,128)(2,1)S(1)} %select_convert_fusion.12), channel_id=1, source_target_pairs={{0,1},{1,0},{2,3},{3,2},{4,5},{5,4},{6,7},{7,6},{8,9},{9,8},{10,11... | collective-permute-start | bytes 786440 | tf_op jit(solution)/shard_map/ppermute | solution.py:16
  314.9 34.6 %collective-permute-start.43 = (bf16[512,1536]{1,0:T(8,128)(2,1)S(1)}, bf16[512,1536]{1,0:T(8,128)(2,1)S(1)}, u32[]{:S(2)}, u32[]{:S(2)}) collective-permute-start(bf16[512,1536]{1,0:T(8,128)(2,1)S(1)} %collective-permute-done.42), channel_id=1, source_target_pairs={{0,8},{8,16},{16,24},{24,28},{28,20},{20,12},{12,4},{4,0},{1,9},{9... | collective-permute-start | bytes 4718600 | tf_op jit(solution)/shard_map/ppermute | solution.py:71
  316.6 34.6 %collective-permute-start.47 = (bf16[512,1536]{1,0:T(8,128)(2,1)S(1)}, bf16[512,1536]{1,0:T(8,128)(2,1)S(1)}, u32[]{:S(2)}, u32[]{:S(2)}) collective-permute-start(bf16[512,1536]{1,0:T(8,128)(2,1)S(1)} %collective-permute-done.46), channel_id=1, source_target_pairs={{8,0},{16,8},{24,16},{28,24},{20,28},{12,20},{4,12},{0,4},{9,1},{1... | collective-permute-start | bytes 4718600 | tf_op jit(solution)/shard_map/ppermute | solution.py:72
  325.6 25.9 %collective-permute-start.41 = (bf16[256,512]{1,0:T(8,128)(2,1)S(1)}, bf16[256,512]{1,0:T(8,128)(2,1)S(1)}, u32[]{:S(2)}, u32[]{:S(2)}) collective-permute-start(bf16[256,512]{1,0:T(8,128)(2,1)S(1)} %pad_maximum_fusion.20), channel_id=1, source_target_pairs={{0,2},{2,0},{1,3},{3,1},{4,6},{6,4},{5,7},{7,5},{8,10},{10,8},{9,1... | collective-permute-start | bytes 786440 | tf_op jit(solution)/shard_map/ppermute | solution.py:16
  325.8 26.0 %collective-permute-start.35 = (bf16[256,1024]{1,0:T(8,128)(2,1)S(1)}, bf16[256,1024]{1,0:T(8,128)(2,1)S(1)}, u32[]{:S(2)}, u32[]{:S(2)}) collective-permute-start(bf16[256,1024]{1,0:T(8,128)(2,1)S(1)} %pad_maximum_fusion.14), channel_id=1, source_target_pairs={{0,2},{2,0},{1,3},{3,1},{4,6},{6,4},{5,7},{7,5},{8,10},{10,8},{9,1... | collective-permute-start | bytes 1572872 | tf_op jit(solution)/shard_map/ppermute | solution.py:16
  349.4 34.5 %collective-permute-start.44 = (bf16[512,1536]{1,0:T(8,128)(2,1)S(1)}, bf16[512,1536]{1,0:T(8,128)(2,1)S(1)}, u32[]{:S(2)}, u32[]{:S(2)}) collective-permute-start(bf16[512,1536]{1,0:T(8,128)(2,1)S(1)} %collective-permute-done.43), channel_id=1, source_target_pairs={{0,8},{8,16},{16,24},{24,28},{28,20},{20,12},{12,4},{4,0},{1,9},{9... | collective-permute-start | bytes 4718600 | tf_op jit(solution)/shard_map/ppermute | solution.py:71
  351.2 34.6 %collective-permute-start.48 = (bf16[512,1536]{1,0:T(8,128)(2,1)S(1)}, bf16[512,1536]{1,0:T(8,128)(2,1)S(1)}, u32[]{:S(2)}, u32[]{:S(2)}) collective-permute-start(bf16[512,1536]{1,0:T(8,128)(2,1)S(1)} %collective-permute-done.47), channel_id=1, source_target_pairs={{8,0},{16,8},{24,16},{28,24},{20,28},{12,20},{4,12},{0,4},{9,1},{1... | collective-permute-start | bytes 4718600 | tf_op jit(solution)/shard_map/ppermute | solution.py:72
  389.6 42.7 %collective-permute-start.52 = (bf16[1024,512]{1,0:T(8,128)(2,1)}, bf16[1024,512]{1,0:T(8,128)(2,1)}, u32[]{:S(2)}, u32[]{:S(2)}) collective-permute-start(bf16[1024,512]{1,0:T(8,128)(2,1)} %get-tuple-element.15), channel_id=1, source_target_pairs={{0,8},{8,16},{16,24},{24,28},{28,20},{20,12},{12,4},{4,0},{1,9},{9... | collective-permute-start | bytes 3145736 | tf_op jit(solution)/shard_map/ppermute | solution.py:71
  391.3 44.5 %collective-permute-start.53 = (bf16[1024,512]{1,0:T(8,128)(2,1)}, bf16[1024,512]{1,0:T(8,128)(2,1)}, u32[]{:S(2)}, u32[]{:S(2)}) collective-permute-start(bf16[1024,512]{1,0:T(8,128)(2,1)} %get-tuple-element.15), channel_id=1, source_target_pairs={{8,0},{16,8},{24,16},{28,24},{20,28},{12,20},{4,12},{0,4},{9,1},{1... | collective-permute-start | bytes 3145736 | tf_op jit(solution)/shard_map/ppermute | solution.py:72
  432.3 25.8 %collective-permute-start.56 = (bf16[1024,512]{1,0:T(8,128)(2,1)}, bf16[1024,512]{1,0:T(8,128)(2,1)S(1)}, u32[]{:S(2)}, u32[]{:S(2)}) collective-permute-start(bf16[1024,512]{1,0:T(8,128)(2,1)} %collective-permute-done.52), channel_id=1, source_target_pairs={{0,8},{8,16},{16,24},{24,28},{28,20},{20,12},{12,4},{4,0},{1,9},{9... | collective-permute-start | bytes 3145736 | tf_op jit(solution)/shard_map/ppermute | solution.py:71
  435.9 25.7 %collective-permute-start.57 = (bf16[1024,512]{1,0:T(8,128)(2,1)}, bf16[1024,512]{1,0:T(8,128)(2,1)S(1)}, u32[]{:S(2)}, u32[]{:S(2)}) collective-permute-start(bf16[1024,512]{1,0:T(8,128)(2,1)} %collective-permute-done.53), channel_id=1, source_target_pairs={{8,0},{16,8},{24,16},{28,24},{20,28},{12,20},{4,12},{0,4},{9,1},{1... | collective-permute-start | bytes 3145736 | tf_op jit(solution)/shard_map/ppermute | solution.py:72
  464.7 25.3 %collective-permute-start.60 = (bf16[1024,512]{1,0:T(8,128)(2,1)S(1)}, bf16[1024,512]{1,0:T(8,128)(2,1)S(1)}, u32[]{:S(2)}, u32[]{:S(2)}) collective-permute-start(bf16[1024,512]{1,0:T(8,128)(2,1)S(1)} %collective-permute-done.56), channel_id=1, source_target_pairs={{0,8},{8,16},{16,24},{24,28},{28,20},{20,12},{12,4},{4,0},{1,9},{9... | collective-permute-start | bytes 3145736 | tf_op jit(solution)/shard_map/ppermute | solution.py:71
  466.5 25.4 %collective-permute-start.61 = (bf16[1024,512]{1,0:T(8,128)(2,1)S(1)}, bf16[1024,512]{1,0:T(8,128)(2,1)S(1)}, u32[]{:S(2)}, u32[]{:S(2)}) collective-permute-start(bf16[1024,512]{1,0:T(8,128)(2,1)S(1)} %collective-permute-done.57), channel_id=1, source_target_pairs={{8,0},{16,8},{24,16},{28,24},{20,28},{12,20},{4,12},{0,4},{9,1},{1... | collective-permute-start | bytes 3145736 | tf_op jit(solution)/shard_map/ppermute | solution.py:72
  (102 other events, 1954.1 us)

commit v2 on v1

--- a/solution.py
+++ b/solution.py
@@ -38,17 +38,18 @@
     return mine + swapped(theirs, axis).astype(F32)
 
 
-def both_layers(own, dim, split):
-    first = lax.axis_index("section") == 0
-    if split:
+def both_layers(shards, dim, splits):
+    section = lax.axis_index("section")
+    mine, give = [], []
+    for own, split in zip(shards, splits):
         half = own.shape[dim] // 2
-        low = lax.slice_in_dim(own, 0, half, axis=dim)
-        high = lax.slice_in_dim(own, half, 2 * half, axis=dim)
-        mine, give = jnp.where(first, low, high), jnp.where(first, high, low)
-    else:
-        mine = give = own
+        for place, kept in ((section, mine), (1 - section, give)):
+            kept.append(
+                lax.dynamic_slice_in_dim(own, place * half, half, dim) if split else own
+            )
+    mine, give = jnp.concatenate(mine, axis=dim), jnp.concatenate(give, axis=dim)
     got = swapped(give, "section")
-    return jnp.where(first, mine, got), jnp.where(first, got, mine)
+    return jnp.where(section == 0, mine, got), jnp.where(section == 0, got, mine)
 
 
 def ring_order(count):
@@ -152,17 +153,11 @@
         return owner * chunk
 
     split = (w_key.shape[2] // HEAD_DIM) % phases == 0
-    query_parts = both_layers(w_query[0], 1, True)
-    kv_parts = both_layers(
-        jnp.stack([w_key[0], w_value[0]], axis=1), 2, split
-    )
-    query_width = query_parts[0].shape[1]
-    key_width = kv_parts[0].shape[2]
-    joined = [
-        jnp.concatenate([q, kv.reshape(kv.shape[0], -1)], axis=1)
-        for q, kv in zip(query_parts, kv_parts)
-    ]
-    out_parts = both_layers(w_out[0], 0, True)
+    joined = both_layers((w_query[0], w_key[0], w_value[0]), 1, (True, split, split))
+    query_width = w_query.shape[2] // phases
+    key_width = w_key.shape[2] // (phases if split else 1)
+    first_ring = ring_gather(joined[0], None)
+    out_parts = both_layers((w_out[0],), 0, (True,))
     first = section == 0
     other_gain = swapped(norm_gain[0], "section")
     gains = (
@@ -188,6 +183,7 @@
     )
     send_ids = jnp.where(filled_flat, segment_ids[chosen], -1).reshape(replicas, capacity)
     send_pos = jnp.where(filled_flat, positions[chosen], 0).reshape(replicas, capacity)
+    send_rows, _ = lax.optimization_barrier((send_rows, first_ring[0][1]))
     got_rows = lax.all_to_all(send_rows, "dp", split_axis=0, concat_axis=0, tiled=True)
     got_marks = lax.all_to_all(
         jnp.concatenate([send_ids, send_pos], axis=1), "dp", split_axis=0, concat_axis=0, tiled=True
@@ -204,7 +200,7 @@
     states = [lax.dynamic_slice_in_dim(packed, s, chunk, 1) for s in starts]
     before = None
     for level in range(phases):
-        projections, before = ring_gather(joined[level], before)
+        projections, before = ring_gather(joined[level], before) if level else first_ring
         outs, before = ring_gather(out_parts[level], before)
         total = sum(
             jnp.sum(jnp.square(piece.astype(F32)), axis=-1, keepdims=True) for piece in states
@@ -215,7 +211,18 @@
             gain = lax.dynamic_slice_in_dim(gains[level], starts[k], chunk, 0)
             normed = (states[k].astype(F32) * inv_scale * gain).astype(BF16)
             projected += jnp.dot(normed, projections[k], preferred_element_type=F32)
-        mixed_heads = attend_local(projected, allowed, factors, query_width, key_width)
+        mixed_heads = []
+        for batch in range(phases):
+            part = projected[batch * row_count : (batch + 1) * row_count]
+            if batch:
+                part, _, _ = lax.optimization_barrier((part, outs[batch], outs[-batch]))
+            one = slice(batch, batch + 1)
+            mixed_heads.append(
+                attend_local(
+                    part, allowed[one], [f[one] for f in factors], query_width, key_width
+                )
+            )
+        mixed_heads = jnp.concatenate(mixed_heads, axis=0)
         fresh = [None] * replicas
         half = replicas // 2
         rounds = [[0]] + [[k, replicas - k] for k in range(1, half)] + [[half]]

time: 529 us -> 581 us (1.098)
  local copies, waits for them, and re-layouts: 45.7 us -> 104 us
  waiting for transfers between devices: 302 us -> 294 us
  other arithmetic: 46.2 us -> 39.1 us
    ppermute x12, waiting for transfers between devices: 48.5 us -> 1.93 us  [ring_gather(): back = lax.ppermute(back, 'dp', left)]
    all_to_all x1, waiting for transfers between devices: 0.05 us -> 27.7 us  [per_device(): lax.all_to_all(jnp.concatenate([send_ids, send_pos], axis=1), 'dp', split...]
    ppermute x12, waiting for transfers between devices: 128 us -> 154 us  [ring_gather(): onward = lax.ppermute(onward, 'dp', right)]
    concatenate x0 -> x8, local copies, waits for them, and re-layouts: none -> 19.3 us  [rotate(): jnp.concatenate([-values[..., half_dim:], values[..., :half_dim]], axis=-1)]
    reshape x4 -> x14, local copies, waits for them, and re-layouts: 5.65 us -> 21 us  [the longest x8 12.4 us: attend_local(): projected[..., query_width:query_width + key_width]]
    ppermute x4, waiting for transfers between devices: 14.9 us -> 1.96 us  [ring_gather(): low = lax.ppermute(back[half:], 'dp', left)]
    sub x2 -> x0, other arithmetic: 7.37 us -> none  [attend_local(): powers = jnp.where(allowed, jnp.exp(scores - row_top), 0.0)]
    ppermute x36 -> x35, waiting for transfers between devices: 59.1 us -> 52.4 us  [swapped(): return lax.ppermute(array, axis, [(0, 1), (1, 0)])]
  transfers between devices with their start and end apart: 70 -> 69, of which waited for: 33 -> 31; matrix products, arithmetic and copies ran while one was open for 26% -> 28% of each run, Pallas kernels for 0% -> 0%
where the time goes in v2:
time: 581 us; the launch traced here: 572 us
  waiting for transfers between devices  294 us (51%)
  local copies, waits for them, and re-layouts  104 us (18%)
  starting transfers between devices  73.4 us (13%)
  matrix products  59.9 us (10%)
  other arithmetic  39.1 us (7%)
    ppermute x12, waiting for transfers between devices, ring_gather(): onward = lax.ppermute(onward, 'dp', right)  154 us
    ppermute x35, waiting for transfers between devices, swapped(): return lax.ppermute(array, axis, [(0, 1), (1, 0)])  52.4 us
    ppermute x4, waiting for transfers between devices, ring_gather(): top = lax.ppermute(onward[:half], 'dp', right)  30.3 us
    all_to_all x1, waiting for transfers between devices, per_device(): lax.all_to_all(jnp.concatenate([send_ids, send_pos], axis=1), 'dp', split...  27.7 us
    dot_general x16, matrix products, per_device(): projected += jnp.dot(normed, projections[k], preferred_element_type=F32)  26 us
    all_to_all x1, waiting for transfers between devices, per_device(): lax.all_to_all(send_rows, 'dp', split_axis=0, concat_axis=0, tiled=True)  25.2 us
    ppermute x35, starting transfers between devices, swapped(): return lax.ppermute(array, axis, [(0, 1), (1, 0)])  21.9 us
    dot_general x16, matrix products, per_device(): jnp.dot(mixed_heads, outs[k], preferred_element_type=F32)  20.2 us
  transfers between devices with their start and end apart: 69, of which 31 were waited for; matrix products, arithmetic and copies ran while one was open for 28% of the time, Pallas kernels for 0%

profile of v2, /device:TPU:0, one launch (start us, length us, event | category | flops | bytes accessed | tf_op | source)
XLA Modules:
  0.0 572.0 jit_solution(12054594896521289266)
XLA Ops:
  2.6 3.2 collective-permute-done
  5.7 3.2 broadcast_select_fusion.3
  9.0 2.9 collective-permute-start.1
  18.9 27.8 %collective-permute-done.1 = bf16[512,1536]{1,0:T(8,128)(2,1)} collective-permute-done((bf16[512,1536]{1,0:T(8,128)(2,1)S(1)}, bf16[512,1536]{1,0:T(8,128)(2,1)}, u32[]{:S(2)}, u32[]{:S(2)}) %collective-permute-start.1) | collective-permute-done | bytes 1572896 | tf_op jit(solution)/shard_map/ppermute | solution.py:72
  46.6 6.1 %all-to-all-start = ((bf16[8,64,1024]{2,1,0:T(8,128)(2,1)}), bf16[8,64,1024]{2,1,0:T(8,128)(2,1)S(1)}, u32[]{:S(2)}, u32[]{:S(2)}) async-start(bf16[8,64,1024]{2,1,0:T(8,128)(2,1)} %broadcast_select_fusion.4), calls=%async_computation | async-start | bytes 2097152 | tf_op jit(solution)/shard_map/all_to_all | solution.py:187
  54.8 25.2 %all-to-all-done = bf16[8,64,1024]{2,1,0:T(8,128)(2,1)S(1)} async-done(((bf16[8,64,1024]{2,1,0:T(8,128)(2,1)}), bf16[8,64,1024]{2,1,0:T(8,128)(2,1)S(1)}, u32[]{:S(2)}, u32[]{:S(2)}) %all-to-all-start) | async-done | bytes 1048608 | tf_op jit(solution)/shard_map/all_to_all | solution.py:187
  84.2 3.5 gather_fusion.1
  87.8 3.5 gather_fusion.2
  91.4 11.6 %collective-permute-done.5 = bf16[512,1536]{1,0:T(8,128)(2,1)} collective-permute-done((bf16[512,1536]{1,0:T(8,128)(2,1)}, bf16[512,1536]{1,0:T(8,128)(2,1)}, u32[]{:S(2)}, u32[]{:S(2)}) %collective-permute-start.5) | collective-permute-done | bytes 1572896 | tf_op jit(solution)/shard_map/ppermute | solution.py:72
  103.0 7.1 %collective-permute-start.6 = (bf16[512,1536]{1,0:T(8,128)(2,1)}, bf16[512,1536]{1,0:T(8,128)(2,1)}, u32[]{:S(2)}, u32[]{:S(2)}) collective-permute-start(bf16[512,1536]{1,0:T(8,128)(2,1)} %collective-permute-done.5), channel_id=1, source_target_pairs={{0,8},{8,16},{16,24},{24,28},{28,20},{20,12},{12,4},{4,0},{1,9},{9... | collective-permute-start | bytes 4718600 | tf_op jit(solution)/shard_map/ppermute | solution.py:72
  113.9 6.3 %all-to-all-start.1 = ((s32[8,1,128]{2,1,0:T(1,128)}), s32[8,1,128]{2,1,0:T(1,128)S(1)}, u32[]{:S(2)}, u32[]{:S(2)}) async-start(s32[8,1,128]{2,1,0:T(1,128)} %bitcast.14), calls=%async_computation.1 | async-start | bytes 8192 | tf_op jit(solution)/shard_map/all_to_all | solution.py:188
  120.5 27.7 %all-to-all-done.1 = s32[8,1,128]{2,1,0:T(1,128)S(1)} async-done(((s32[8,1,128]{2,1,0:T(1,128)}), s32[8,1,128]{2,1,0:T(1,128)S(1)}, u32[]{:S(2)}, u32[]{:S(2)}) %all-to-all-start.1) | async-done | bytes 4128 | tf_op jit(solution)/shard_map/all_to_all | solution.py:188
  162.0 15.3 %collective-permute-done.13 = bf16[1024,512]{1,0:T(8,128)(2,1)} collective-permute-done((bf16[1024,512]{1,0:T(8,128)(2,1)S(1)}, bf16[1024,512]{1,0:T(8,128)(2,1)}, u32[]{:S(2)}, u32[]{:S(2)}) %collective-permute-start.13) | collective-permute-done | bytes 1048608 | tf_op jit(solution)/shard_map/ppermute | solution.py:72
  243.9 2.9 fusion.6
  267.7 6.8 %collective-permute-done.20 = bf16[128,1024]{1,0:T(8,128)(2,1)S(1)} collective-permute-done((bf16[128,1024]{1,0:T(8,128)(2,1)S(1)}, bf16[128,1024]{1,0:T(8,128)(2,1)S(1)}, u32[]{:S(2)}, u32[]{:S(2)}) %collective-permute-start.20) | collective-permute-done | bytes 262176 | tf_op jit(solution)/shard_map/ppermute | solution.py:16
  276.8 3.3 collective-permute-done.26
  281.8 3.9 collective-permute-done.21
  294.6 8.7 %collective-permute-done.35 = bf16[512,512]{1,0:T(8,128)(2,1)S(1)} collective-permute-done((bf16[512,512]{1,0:T(8,128)(2,1)S(1)}, bf16[512,512]{1,0:T(8,128)(2,1)S(1)}, u32[]{:S(2)}, u32[]{:S(2)}) %collective-permute-start.35) | collective-permute-done | bytes 524320 | tf_op jit(solution)/shard_map/ppermute | solution.py:76
  310.0 8.5 %collective-permute-done.38 = bf16[128,512]{1,0:T(8,128)(2,1)S(1)} collective-permute-done((bf16[128,512]{1,0:T(8,128)(2,1)S(1)}, bf16[128,512]{1,0:T(8,128)(2,1)S(1)}, u32[]{:S(2)}, u32[]{:S(2)}) %collective-permute-start.38) | collective-permute-done | bytes 131104 | tf_op jit(solution)/shard_map/ppermute | solution.py:16
  320.5 15.2 %collective-permute-done.41 = bf16[512,1536]{1,0:T(8,128)(2,1)S(1)} collective-permute-done((bf16[512,1536]{1,0:T(8,128)(2,1)S(1)}, bf16[512,1536]{1,0:T(8,128)(2,1)S(1)}, u32[]{:S(2)}, u32[]{:S(2)}) %collective-permute-start.41) | collective-permute-done | bytes 1572896 | tf_op jit(solution)/shard_map/ppermute | solution.py:72
  340.7 6.5 %collective-permute-done.39 = bf16[128,512]{1,0:T(8,128)(2,1)S(1)} collective-permute-done((bf16[128,512]{1,0:T(8,128)(2,1)S(1)}, bf16[128,512]{1,0:T(8,128)(2,1)S(1)}, u32[]{:S(2)}, u32[]{:S(2)}) %collective-permute-start.39) | collective-permute-done | bytes 131104 | tf_op jit(solution)/shard_map/ppermute | solution.py:16
  348.3 22.5 %collective-permute-done.42 = bf16[512,1536]{1,0:T(8,128)(2,1)S(1)} collective-permute-done((bf16[512,1536]{1,0:T(8,128)(2,1)S(1)}, bf16[512,1536]{1,0:T(8,128)(2,1)S(1)}, u32[]{:S(2)}, u32[]{:S(2)}) %collective-permute-start.42) | collective-permute-done | bytes 1572896 | tf_op jit(solution)/shard_map/ppermute | solution.py:72
  375.8 29.4 %collective-permute-done.43 = bf16[512,1536]{1,0:T(8,128)(2,1)S(1)} collective-permute-done((bf16[512,1536]{1,0:T(8,128)(2,1)S(1)}, bf16[512,1536]{1,0:T(8,128)(2,1)S(1)}, u32[]{:S(2)}, u32[]{:S(2)}) %collective-permute-start.43) | collective-permute-done | bytes 1572896 | tf_op jit(solution)/shard_map/ppermute | solution.py:72
  412.9 12.9 %collective-permute-done.44 = bf16[256,1536]{1,0:T(8,128)(2,1)S(1)} collective-permute-done((bf16[256,1536]{1,0:T(8,128)(2,1)S(1)}, bf16[256,1536]{1,0:T(8,128)(2,1)S(1)}, u32[]{:S(2)}, u32[]{:S(2)}) %collective-permute-start.44) | collective-permute-done | bytes 786464 | tf_op jit(solution)/shard_map/ppermute | solution.py:76
  454.5 2.9 fusion.8
  480.2 2.9 fusion.9
  495.3 17.6 %collective-permute-done.55 = bf16[1024,512]{1,0:T(8,128)(2,1)S(1)} collective-permute-done((bf16[1024,512]{1,0:T(8,128)(2,1)}, bf16[1024,512]{1,0:T(8,128)(2,1)S(1)}, u32[]{:S(2)}, u32[]{:S(2)}) %collective-permute-start.55) | collective-permute-done | bytes 1048608 | tf_op jit(solution)/shard_map/ppermute | solution.py:72
  521.3 4.8 collective-permute-done.54
  526.3 4.2 collective-permute-done.58
  530.8 12.2 %collective-permute-done.59 = bf16[1024,512]{1,0:T(8,128)(2,1)S(1)} collective-permute-done((bf16[1024,512]{1,0:T(8,128)(2,1)S(1)}, bf16[1024,512]{1,0:T(8,128)(2,1)S(1)}, u32[]{:S(2)}, u32[]{:S(2)}) %collective-permute-start.59) | collective-permute-done | bytes 1048608 | tf_op jit(solution)/shard_map/ppermute | solution.py:72
  547.0 8.7 %collective-permute-done.63 = bf16[512,512]{1,0:T(8,128)(2,1)S(1)} collective-permute-done((bf16[512,512]{1,0:T(8,128)(2,1)S(1)}, bf16[512,512]{1,0:T(8,128)(2,1)S(1)}, u32[]{:S(2)}, u32[]{:S(2)}) %collective-permute-start.63) | collective-permute-done | bytes 524320 | tf_op jit(solution)/shard_map/ppermute | solution.py:76
  560.5 6.8 %collective-permute-done.62 = bf16[128,1024]{1,0:T(8,128)(2,1)S(1)} collective-permute-done((bf16[128,1024]{1,0:T(8,128)(2,1)S(1)}, bf16[128,1024]{1,0:T(8,128)(2,1)S(1)}, u32[]{:S(2)}, u32[]{:S(2)}) %collective-permute-start.62) | collective-permute-done | bytes 262176 | tf_op jit(solution)/shard_map/ppermute | solution.py:16
  (462 shorter events, 245.7 us)
Async XLA Ops:
  9.0 37.7 %collective-permute-start.1 = (bf16[512,1536]{1,0:T(8,128)(2,1)S(1)}, bf16[512,1536]{1,0:T(8,128)(2,1)}, u32[]{:S(2)}, u32[]{:S(2)}) collective-permute-start(bf16[512,1536]{1,0:T(8,128)(2,1)S(1)} %get-tuple-element.67), channel_id=1, source_target_pairs={{0,8},{8,16},{16,24},{24,28},{28,20},{20,12},{12,4},{4,0},{1,9},{9... | collective-permute-start | bytes 4718600 | tf_op jit(solution)/shard_map/ppermute | solution.py:72
  16.4 38.3 %collective-permute-start.8 = (bf16[512,1536]{1,0:T(8,128)(2,1)S(1)}, bf16[512,1536]{1,0:T(8,128)(2,1)}, u32[]{:S(2)}, u32[]{:S(2)}) collective-permute-start(bf16[512,1536]{1,0:T(8,128)(2,1)S(1)} %get-tuple-element.67), channel_id=1, source_target_pairs={{8,0},{16,8},{24,16},{28,24},{20,28},{12,20},{4,12},{0,4},{9,1},{1... | collective-permute-start | bytes 4718600 | tf_op jit(solution)/shard_map/ppermute | solution.py:73
  46.6 33.3 %all-to-all-start = ((bf16[8,64,1024]{2,1,0:T(8,128)(2,1)}), bf16[8,64,1024]{2,1,0:T(8,128)(2,1)S(1)}, u32[]{:S(2)}, u32[]{:S(2)}) async-start(bf16[8,64,1024]{2,1,0:T(8,128)(2,1)} %broadcast_select_fusion.4), calls=%async_computation | async-start | bytes 2097152 | tf_op jit(solution)/shard_map/all_to_all | solution.py:187
  52.7 50.3 %collective-permute-start.5 = (bf16[512,1536]{1,0:T(8,128)(2,1)}, bf16[512,1536]{1,0:T(8,128)(2,1)}, u32[]{:S(2)}, u32[]{:S(2)}) collective-permute-start(bf16[512,1536]{1,0:T(8,128)(2,1)} %collective-permute-done.1), channel_id=1, source_target_pairs={{0,8},{8,16},{16,24},{24,28},{28,20},{20,12},{12,4},{4,0},{1,9},{9... | collective-permute-start | bytes 4718600 | tf_op jit(solution)/shard_map/ppermute | solution.py:72
  54.7 55.4 %collective-permute-start.9 = (bf16[512,1536]{1,0:T(8,128)(2,1)}, bf16[512,1536]{1,0:T(8,128)(2,1)}, u32[]{:S(2)}, u32[]{:S(2)}) collective-permute-start(bf16[512,1536]{1,0:T(8,128)(2,1)} %collective-permute-done.8), channel_id=1, source_target_pairs={{8,0},{16,8},{24,16},{28,24},{20,28},{12,20},{4,12},{0,4},{9,1},{1... | collective-permute-start | bytes 4718600 | tf_op jit(solution)/shard_map/ppermute | solution.py:73
  79.9 30.2 %collective-permute-start.2 = (bf16[512,1024]{1,0:T(8,128)(2,1)S(1)}, bf16[512,1024]{1,0:T(8,128)(2,1)}, u32[]{:S(2)}, u32[]{:S(2)}) collective-permute-start(bf16[512,1024]{1,0:T(8,128)(2,1)S(1)} %bitcast.253), channel_id=1, source_target_pairs={{0,1},{1,0},{2,3},{3,2},{4,5},{5,4},{6,7},{7,6},{8,9},{9,8},{10,11... | collective-permute-start | bytes 3145736 | tf_op jit(solution)/shard_map/ppermute | solution.py:16
  81.5 74.4 %collective-permute-start.4 = (f32[4096]{0:T(1024)}, f32[4096]{0:T(1024)}, u32[]{:S(2)}, u32[]{:S(2)}) collective-permute-start(f32[4096]{0:T(1024)} %bitcast.9), channel_id=1, source_target_pairs={{0,2},{2,0},{1,3},{3,1},{4,6},{6,4},{5,7},{7,5},{8,10},{10,8},{9,1... | collective-permute-start | bytes 49160 | tf_op jit(solution)/shard_map/ppermute | solution.py:16
  83.7 64.7 %collective-permute-start.12 = (bf16[1024,512]{1,0:T(8,128)(2,1)}, bf16[1024,512]{1,0:T(8,128)(2,1)}, u32[]{:S(2)}, u32[]{:S(2)}) collective-permute-start(bf16[1024,512]{1,0:T(8,128)(2,1)} %dynamic-slice_bitcast_fusion), channel_id=1, source_target_pairs={{0,2},{2,0},{1,3},{3,1},{4,6},{6,4},{5,7},{7,5},{8,10},{10,8},{9,1... | collective-permute-start | bytes 3145736 | tf_op jit(solution)/shard_map/ppermute | solution.py:16
  103.0 48.1 %collective-permute-start.6 = (bf16[512,1536]{1,0:T(8,128)(2,1)}, bf16[512,1536]{1,0:T(8,128)(2,1)}, u32[]{:S(2)}, u32[]{:S(2)}) collective-permute-start(bf16[512,1536]{1,0:T(8,128)(2,1)} %collective-permute-done.5), channel_id=1, source_target_pairs={{0,8},{8,16},{16,24},{24,28},{28,20},{20,12},{12,4},{4,0},{1,9},{9... | collective-permute-start | bytes 4718600 | tf_op jit(solution)/shard_map/ppermute | solution.py:72
  110.1 41.0 %collective-permute-start.10 = (bf16[512,1536]{1,0:T(8,128)(2,1)}, bf16[512,1536]{1,0:T(8,128)(2,1)}, u32[]{:S(2)}, u32[]{:S(2)}) collective-permute-start(bf16[512,1536]{1,0:T(8,128)(2,1)} %collective-permute-done.9), channel_id=1, source_target_pairs={{8,0},{16,8},{24,16},{28,24},{20,28},{12,20},{4,12},{0,4},{9,1},{1... | collective-permute-start | bytes 4718600 | tf_op jit(solution)/shard_map/ppermute | solution.py:73
  113.2 66.2 %collective-permute-start.3 = (bf16[512,2048]{1,0:T(8,128)(2,1)}, bf16[512,2048]{1,0:T(8,128)(2,1)}, u32[]{:S(2)}, u32[]{:S(2)}) collective-permute-start(bf16[512,2048]{1,0:T(8,128)(2,1)} %pad_maximum_fusion), channel_id=1, source_target_pairs={{0,2},{2,0},{1,3},{3,1},{4,6},{6,4},{5,7},{7,5},{8,10},{10,8},{9,1... | collective-permute-start | bytes 6291464 | tf_op jit(solution)/shard_map/ppermute | solution.py:16
  113.9 34.3 %all-to-all-start.1 = ((s32[8,1,128]{2,1,0:T(1,128)}), s32[8,1,128]{2,1,0:T(1,128)S(1)}, u32[]{:S(2)}, u32[]{:S(2)}) async-start(s32[8,1,128]{2,1,0:T(1,128)} %bitcast.14), calls=%async_computation.1 | async-start | bytes 8192 | tf_op jit(solution)/shard_map/all_to_all | solution.py:188
  151.1 26.3 %collective-permute-start.13 = (bf16[1024,512]{1,0:T(8,128)(2,1)S(1)}, bf16[1024,512]{1,0:T(8,128)(2,1)}, u32[]{:S(2)}, u32[]{:S(2)}) collective-permute-start(bf16[1024,512]{1,0:T(8,128)(2,1)S(1)} %get-tuple-element.16), channel_id=1, source_target_pairs={{0,8},{8,16},{16,24},{24,28},{28,20},{20,12},{12,4},{4,0},{1,9},{9... | collective-permute-start | bytes 3145736 | tf_op jit(solution)/shard_map/ppermute | solution.py:72
  151.7 26.2 %collective-permute-start.14 = (bf16[1024,512]{1,0:T(8,128)(2,1)S(1)}, bf16[1024,512]{1,0:T(8,128)(2,1)}, u32[]{:S(2)}, u32[]{:S(2)}) collective-permute-start(bf16[1024,512]{1,0:T(8,128)(2,1)S(1)} %get-tuple-element.16), channel_id=1, source_target_pairs={{8,0},{16,8},{24,16},{28,24},{20,28},{12,20},{4,12},{0,4},{9,1},{1... | collective-permute-start | bytes 3145736 | tf_op jit(solution)/shard_map/ppermute | solution.py:73
  158.7 37.3 %collective-permute-start.7 = (bf16[256,1536]{1,0:T(8,128)(2,1)S(1)}, bf16[256,1536]{1,0:T(8,128)(2,1)S(1)}, u32[]{:S(2)}, u32[]{:S(2)}) collective-permute-start(bf16[256,1536]{1,0:T(8,128)(2,1)S(1)} %slice.463), channel_id=1, source_target_pairs={{0,8},{8,16},{16,24},{24,28},{28,20},{20,12},{12,4},{4,0},{1,9},{9... | collective-permute-start | bytes 2359304 | tf_op jit(solution)/shard_map/ppermute | solution.py:76
  160.5 35.5 %collective-permute-start.11 = (bf16[256,1536]{1,0:T(8,128)(2,1)S(1)}, bf16[256,1536]{1,0:T(8,128)(2,1)S(1)}, u32[]{:S(2)}, u32[]{:S(2)}) collective-permute-start(bf16[256,1536]{1,0:T(8,128)(2,1)S(1)} %slice.464), channel_id=1, source_target_pairs={{8,0},{16,8},{24,16},{28,24},{20,28},{12,20},{4,12},{0,4},{9,1},{1... | collective-permute-start | bytes 2359304 | tf_op jit(solution)/shard_map/ppermute | solution.py:77
  177.3 81.2 %collective-permute-start.23 = (bf16[1024,512]{1,0:T(8,128)(2,1)}, bf16[1024,512]{1,0:T(8,128)(2,1)}, u32[]{:S(2)}, u32[]{:S(2)}) collective-permute-start(bf16[1024,512]{1,0:T(8,128)(2,1)} %collective-permute-done.13), channel_id=1, source_target_pairs={{0,8},{8,16},{16,24},{24,28},{28,20},{20,12},{12,4},{4,0},{1,9},{9... | collective-permute-start | bytes 3145736 | tf_op jit(solution)/shard_map/ppermute | solution.py:72
  177.9 82.5 %collective-permute-start.24 = (bf16[1024,512]{1,0:T(8,128)(2,1)}, bf16[1024,512]{1,0:T(8,128)(2,1)}, u32[]{:S(2)}, u32[]{:S(2)}) collective-permute-start(bf16[1024,512]{1,0:T(8,128)(2,1)} %collective-permute-done.14), channel_id=1, source_target_pairs={{8,0},{16,8},{24,16},{28,24},{20,28},{12,20},{4,12},{0,4},{9,1},{1... | collective-permute-start | bytes 3145736 | tf_op jit(solution)/shard_map/ppermute | solution.py:73
  262.7 25.8 %collective-permute-start.29 = (bf16[1024,512]{1,0:T(8,128)(2,1)}, bf16[1024,512]{1,0:T(8,128)(2,1)S(1)}, u32[]{:S(2)}, u32[]{:S(2)}) collective-permute-start(bf16[1024,512]{1,0:T(8,128)(2,1)} %collective-permute-done.23), channel_id=1, source_target_pairs={{0,8},{8,16},{16,24},{24,28},{28,20},{20,12},{12,4},{4,0},{1,9},{9... | collective-permute-start | bytes 3145736 | tf_op jit(solution)/shard_map/ppermute | solution.py:72
  263.3 25.8 %collective-permute-start.30 = (bf16[1024,512]{1,0:T(8,128)(2,1)}, bf16[1024,512]{1,0:T(8,128)(2,1)S(1)}, u32[]{:S(2)}, u32[]{:S(2)}) collective-permute-start(bf16[1024,512]{1,0:T(8,128)(2,1)} %collective-permute-done.24), channel_id=1, source_target_pairs={{8,0},{16,8},{24,16},{28,24},{20,28},{12,20},{4,12},{0,4},{9,1},{1... | collective-permute-start | bytes 3145736 | tf_op jit(solution)/shard_map/ppermute | solution.py:73
  276.2 33.8 %collective-permute-start.16 = (bf16[128,512]{1,0:T(8,128)(2,1)S(1)}, bf16[128,512]{1,0:T(8,128)(2,1)S(1)}, u32[]{:S(2)}, u32[]{:S(2)}) collective-permute-start(bf16[128,512]{1,0:T(8,128)(2,1)S(1)} %select_convert_fusion.19), channel_id=1, source_target_pairs={{0,1},{1,0},{2,3},{3,2},{4,5},{5,4},{6,7},{7,6},{8,9},{9,8},{10,11... | collective-permute-start | bytes 393224 | tf_op jit(solution)/shard_map/ppermute | solution.py:16
  293.5 42.2 %collective-permute-start.41 = (bf16[512,1536]{1,0:T(8,128)(2,1)S(1)}, bf16[512,1536]{1,0:T(8,128)(2,1)S(1)}, u32[]{:S(2)}, u32[]{:S(2)}) collective-permute-start(bf16[512,1536]{1,0:T(8,128)(2,1)S(1)} %copy-done.17), channel_id=1, source_target_pairs={{0,8},{8,16},{16,24},{24,28},{28,20},{20,12},{12,4},{4,0},{1,9},{9... | collective-permute-start | bytes 4718600 | tf_op jit(solution)/shard_map/ppermute | solution.py:72
  303.4 33.9 %collective-permute-start.45 = (bf16[512,1536]{1,0:T(8,128)(2,1)S(1)}, bf16[512,1536]{1,0:T(8,128)(2,1)S(1)}, u32[]{:S(2)}, u32[]{:S(2)}) collective-permute-start(bf16[512,1536]{1,0:T(8,128)(2,1)S(1)} %copy-done.17), channel_id=1, source_target_pairs={{8,0},{16,8},{24,16},{28,24},{20,28},{12,20},{4,12},{0,4},{9,1},{1... | collective-permute-start | bytes 4718600 | tf_op jit(solution)/shard_map/ppermute | solution.py:73
  307.1 31.2 %collective-permute-start.32 = (bf16[128,1024]{1,0:T(8,128)(2,1)S(1)}, bf16[128,1024]{1,0:T(8,128)(2,1)S(1)}, u32[]{:S(2)}, u32[]{:S(2)}) collective-permute-start(bf16[128,1024]{1,0:T(8,128)(2,1)S(1)} %select_convert_fusion.12), channel_id=1, source_target_pairs={{0,1},{1,0},{2,3},{3,2},{4,5},{5,4},{6,7},{7,6},{8,9},{9,8},{10,11... | collective-permute-start | bytes 786440 | tf_op jit(solution)/shard_map/ppermute | solution.py:16
  335.7 35.1 %collective-permute-start.42 = (bf16[512,1536]{1,0:T(8,128)(2,1)S(1)}, bf16[512,1536]{1,0:T(8,128)(2,1)S(1)}, u32[]{:S(2)}, u32[]{:S(2)}) collective-permute-start(bf16[512,1536]{1,0:T(8,128)(2,1)S(1)} %collective-permute-done.41), channel_id=1, source_target_pairs={{0,8},{8,16},{16,24},{24,28},{28,20},{20,12},{12,4},{4,0},{1,9},{9... | collective-permute-start | bytes 4718600 | tf_op jit(solution)/shard_map/ppermute | solution.py:72
  337.2 34.1 %collective-permute-start.46 = (bf16[512,1536]{1,0:T(8,128)(2,1)S(1)}, bf16[512,1536]{1,0:T(8,128)(2,1)S(1)}, u32[]{:S(2)}, u32[]{:S(2)}) collective-permute-start(bf16[512,1536]{1,0:T(8,128)(2,1)S(1)} %collective-permute-done.45), channel_id=1, source_target_pairs={{8,0},{16,8},{24,16},{28,24},{20,28},{12,20},{4,12},{0,4},{9,1},{1... | collective-permute-start | bytes 4718600 | tf_op jit(solution)/shard_map/ppermute | solution.py:73
  347.4 25.7 %collective-permute-start.34 = (bf16[256,1024]{1,0:T(8,128)(2,1)S(1)}, bf16[256,1024]{1,0:T(8,128)(2,1)S(1)}, u32[]{:S(2)}, u32[]{:S(2)}) collective-permute-start(bf16[256,1024]{1,0:T(8,128)(2,1)S(1)} %pad_maximum_fusion.15), channel_id=1, source_target_pairs={{0,2},{2,0},{1,3},{3,1},{4,6},{6,4},{5,7},{7,5},{8,10},{10,8},{9,1... | collective-permute-start | bytes 1572872 | tf_op jit(solution)/shard_map/ppermute | solution.py:16
  370.8 34.5 %collective-permute-start.43 = (bf16[512,1536]{1,0:T(8,128)(2,1)S(1)}, bf16[512,1536]{1,0:T(8,128)(2,1)S(1)}, u32[]{:S(2)}, u32[]{:S(2)}) collective-permute-start(bf16[512,1536]{1,0:T(8,128)(2,1)S(1)} %collective-permute-done.42), channel_id=1, source_target_pairs={{0,8},{8,16},{16,24},{24,28},{28,20},{20,12},{12,4},{4,0},{1,9},{9... | collective-permute-start | bytes 4718600 | tf_op jit(solution)/shard_map/ppermute | solution.py:72
  371.4 34.6 %collective-permute-start.47 = (bf16[512,1536]{1,0:T(8,128)(2,1)S(1)}, bf16[512,1536]{1,0:T(8,128)(2,1)S(1)}, u32[]{:S(2)}, u32[]{:S(2)}) collective-permute-start(bf16[512,1536]{1,0:T(8,128)(2,1)S(1)} %collective-permute-done.46), channel_id=1, source_target_pairs={{8,0},{16,8},{24,16},{28,24},{20,28},{12,20},{4,12},{0,4},{9,1},{1... | collective-permute-start | bytes 4718600 | tf_op jit(solution)/shard_map/ppermute | solution.py:73
  410.7 49.2 %collective-permute-start.49 = (bf16[1024,512]{1,0:T(8,128)(2,1)}, bf16[1024,512]{1,0:T(8,128)(2,1)}, u32[]{:S(2)}, u32[]{:S(2)}) collective-permute-start(bf16[1024,512]{1,0:T(8,128)(2,1)} %get-tuple-element.21), channel_id=1, source_target_pairs={{0,8},{8,16},{16,24},{24,28},{28,20},{20,12},{12,4},{4,0},{1,9},{9... | collective-permute-start | bytes 3145736 | tf_op jit(solution)/shard_map/ppermute | solution.py:72
  411.3 48.6 %collective-permute-start.50 = (bf16[1024,512]{1,0:T(8,128)(2,1)}, bf16[1024,512]{1,0:T(8,128)(2,1)}, u32[]{:S(2)}, u32[]{:S(2)}) collective-permute-start(bf16[1024,512]{1,0:T(8,128)(2,1)} %get-tuple-element.21), channel_id=1, source_target_pairs={{8,0},{16,8},{24,16},{28,24},{20,28},{12,20},{4,12},{0,4},{9,1},{1... | collective-permute-start | bytes 3145736 | tf_op jit(solution)/shard_map/ppermute | solution.py:73
  487.1 25.8 %collective-permute-start.55 = (bf16[1024,512]{1,0:T(8,128)(2,1)}, bf16[1024,512]{1,0:T(8,128)(2,1)S(1)}, u32[]{:S(2)}, u32[]{:S(2)}) collective-permute-start(bf16[1024,512]{1,0:T(8,128)(2,1)} %collective-permute-done.49), channel_id=1, source_target_pairs={{0,8},{8,16},{16,24},{24,28},{28,20},{20,12},{12,4},{4,0},{1,9},{9... | collective-permute-start | bytes 3145736 | tf_op jit(solution)/shard_map/ppermute | solution.py:72
  (107 other events, 1494.2 us)

commit v3 on v2

--- a/solution.py
+++ b/solution.py
@@ -183,11 +183,11 @@
     )
     send_ids = jnp.where(filled_flat, segment_ids[chosen], -1).reshape(replicas, capacity)
     send_pos = jnp.where(filled_flat, positions[chosen], 0).reshape(replicas, capacity)
-    send_rows, _ = lax.optimization_barrier((send_rows, first_ring[0][1]))
-    got_rows = lax.all_to_all(send_rows, "dp", split_axis=0, concat_axis=0, tiled=True)
     got_marks = lax.all_to_all(
         jnp.concatenate([send_ids, send_pos], axis=1), "dp", split_axis=0, concat_axis=0, tiled=True
     )
+    send_rows, _, got_marks = lax.optimization_barrier((send_rows, first_ring[0][1], got_marks))
+    got_rows = lax.all_to_all(send_rows, "dp", split_axis=0, concat_axis=0, tiled=True)
     packed = join(join(got_rows.reshape(packed_len, share), "tensor", 1), "section", 1)
     id_rows = got_marks[:, :capacity].reshape(phases, row_count)
     pos_rows = got_marks[:, capacity:].reshape(phases, row_count)
@@ -211,18 +211,7 @@
             gain = lax.dynamic_slice_in_dim(gains[level], starts[k], chunk, 0)
             normed = (states[k].astype(F32) * inv_scale * gain).astype(BF16)
             projected += jnp.dot(normed, projections[k], preferred_element_type=F32)
-        mixed_heads = []
-        for batch in range(phases):
-            part = projected[batch * row_count : (batch + 1) * row_count]
-            if batch:
-                part, _, _ = lax.optimization_barrier((part, outs[batch], outs[-batch]))
-            one = slice(batch, batch + 1)
-            mixed_heads.append(
-                attend_local(
-                    part, allowed[one], [f[one] for f in factors], query_width, key_width
-                )
-            )
-        mixed_heads = jnp.concatenate(mixed_heads, axis=0)
+        mixed_heads = attend_local(projected, allowed, factors, query_width, key_width)
         fresh = [None] * replicas
         half = replicas // 2
         rounds = [[0]] + [[k, replicas - k] for k in range(1, half)] + [[half]]

time: 581 us -> 521 us (0.90)
  local copies, waits for them, and re-layouts: 104 us -> 42.1 us
    ppermute x12, waiting for transfers between devices: 1.93 us -> 33.3 us  [ring_gather(): back = lax.ppermute(back, 'dp', left)]
    concatenate x8 -> x0, local copies, waits for them, and re-layouts: 19.3 us -> none  [rotate(): jnp.concatenate([-values[..., half_dim:], values[..., :half_dim]], axis=-1)]
    reshape x14 -> x2, local copies, waits for them, and re-layouts: 21 us -> 2.75 us  [attend_local(): return mixed_heads.astype(BF16).reshape(batches * row_len, query_width)]
    all_to_all x1, waiting for transfers between devices: 27.7 us -> 16.3 us  [per_device(): lax.all_to_all(jnp.concatenate([send_ids, send_pos], axis=1), 'dp', split...]
    ppermute x12, waiting for transfers between devices: 154 us -> 144 us  [ring_gather(): onward = lax.ppermute(onward, 'dp', right)]
    all_to_all x1, waiting for transfers between devices: 25.2 us -> 17.6 us  [per_device(): lax.all_to_all(send_rows, 'dp', split_axis=0, concat_axis=0, tiled=True)]
    another operation x4 -> x0, local copies, waits for them, and re-layouts: 6.65 us -> none
    slice x4 -> x0, local copies, waits for them, and re-layouts: 6.09 us -> none  [rotate(): values[..., half_dim:]]
  transfers between devices with their start and end apart: 69 -> 69, of which waited for: 31 -> 34; matrix products, arithmetic and copies ran while one was open for 28% -> 25% of each run, Pallas kernels for 0% -> 0%
where the time goes in v3:
time: 521 us; the launch traced here: 515 us
  waiting for transfers between devices  298 us (57%)
  starting transfers between devices  77.2 us (15%)
  matrix products  56.4 us (11%)
  local copies, waits for them, and re-layouts  42.1 us (8%)
  other arithmetic  38.9 us (7%)
    ppermute x12, waiting for transfers between devices, ring_gather(): onward = lax.ppermute(onward, 'dp', right)  144 us
    ppermute x35, waiting for transfers between devices, swapped(): return lax.ppermute(array, axis, [(0, 1), (1, 0)])  55.4 us
    ppermute x12, waiting for transfers between devices, ring_gather(): back = lax.ppermute(back, 'dp', left)  33.3 us
    ppermute x4, waiting for transfers between devices, ring_gather(): top = lax.ppermute(onward[:half], 'dp', right)  29.2 us
    ppermute x12, starting transfers between devices, ring_gather(): onward = lax.ppermute(onward, 'dp', right)  25.2 us
    dot_general x16, matrix products, per_device(): projected += jnp.dot(normed, projections[k], preferred_element_type=F32)  24.6 us
    ppermute x35, starting transfers between devices, swapped(): return lax.ppermute(array, axis, [(0, 1), (1, 0)])  22 us
    dot_general x16, matrix products, per_device(): jnp.dot(mixed_heads, outs[k], preferred_element_type=F32)  21.6 us
  transfers between devices with their start and end apart: 69, of which 34 were waited for; matrix products, arithmetic and copies ran while one was open for 25% of the time, Pallas kernels for 0%

profile of v3, /device:TPU:0, one launch (start us, length us, event | category | flops | bytes accessed | tf_op | source)
XLA Modules:
  0.0 514.8 jit_solution(6539475185806031269)
XLA Ops:
  12.2 3.5 gather_fusion.1
  15.8 3.5 gather_fusion.2
  20.2 4.8 all-to-all-start
  33.5 16.3 %all-to-all-done = s32[8,1,128]{2,1,0:T(1,128)S(1)} async-done(((s32[8,1,128]{2,1,0:T(1,128)}), s32[8,1,128]{2,1,0:T(1,128)S(1)}, u32[]{:S(2)}, u32[]{:S(2)}) %all-to-all-start) | async-done | bytes 4128 | tf_op jit(solution)/shard_map/all_to_all | solution.py:186
  49.7 3.6 all-to-all-start.1
  55.2 14.6 %collective-permute-done.8 = bf16[512,1536]{1,0:T(8,128)(2,1)} collective-permute-done((bf16[512,1536]{1,0:T(8,128)(2,1)S(1)}, bf16[512,1536]{1,0:T(8,128)(2,1)}, u32[]{:S(2)}, u32[]{:S(2)}) %collective-permute-start.8) | collective-permute-done | bytes 1572896 | tf_op jit(solution)/shard_map/ppermute | solution.py:73
  72.7 17.6 %all-to-all-done.1 = bf16[8,64,1024]{2,1,0:T(8,128)(2,1)S(1)} async-done(((bf16[8,64,1024]{2,1,0:T(8,128)(2,1)}), bf16[8,64,1024]{2,1,0:T(8,128)(2,1)S(1)}, u32[]{:S(2)}, u32[]{:S(2)}) %all-to-all-start.1) | async-done | bytes 1048608 | tf_op jit(solution)/shard_map/all_to_all | solution.py:190
  91.9 11.7 %collective-permute-done.5 = bf16[512,1536]{1,0:T(8,128)(2,1)} collective-permute-done((bf16[512,1536]{1,0:T(8,128)(2,1)}, bf16[512,1536]{1,0:T(8,128)(2,1)}, u32[]{:S(2)}, u32[]{:S(2)}) %collective-permute-start.5) | collective-permute-done | bytes 1572896 | tf_op jit(solution)/shard_map/ppermute | solution.py:72
  103.5 7.1 %collective-permute-start.6 = (bf16[512,1536]{1,0:T(8,128)(2,1)}, bf16[512,1536]{1,0:T(8,128)(2,1)S(1)}, u32[]{:S(2)}, u32[]{:S(2)}) collective-permute-start(bf16[512,1536]{1,0:T(8,128)(2,1)} %collective-permute-done.5), channel_id=1, source_target_pairs={{0,8},{8,16},{16,24},{24,28},{28,20},{20,12},{12,4},{4,0},{1,9},{9... | collective-permute-start | bytes 4718600 | tf_op jit(solution)/shard_map/ppermute | solution.py:72
  110.7 4.9 collective-permute-done.9
  122.8 3.4 collective-permute-done.4
  129.5 14.8 %collective-permute-done.6 = bf16[512,1536]{1,0:T(8,128)(2,1)S(1)} collective-permute-done((bf16[512,1536]{1,0:T(8,128)(2,1)}, bf16[512,1536]{1,0:T(8,128)(2,1)S(1)}, u32[]{:S(2)}, u32[]{:S(2)}) %collective-permute-start.6) | collective-permute-done | bytes 1572896 | tf_op jit(solution)/shard_map/ppermute | solution.py:72
  144.3 11.9 %collective-permute-done.10 = bf16[512,1536]{1,0:T(8,128)(2,1)} collective-permute-done((bf16[512,1536]{1,0:T(8,128)(2,1)}, bf16[512,1536]{1,0:T(8,128)(2,1)}, u32[]{:S(2)}, u32[]{:S(2)}) %collective-permute-start.10) | collective-permute-done | bytes 1572896 | tf_op jit(solution)/shard_map/ppermute | solution.py:73
  164.8 17.9 %collective-permute-done.17 = bf16[1024,512]{1,0:T(8,128)(2,1)} collective-permute-done((bf16[1024,512]{1,0:T(8,128)(2,1)}, bf16[1024,512]{1,0:T(8,128)(2,1)}, u32[]{:S(2)}, u32[]{:S(2)}) %collective-permute-start.17) | collective-permute-done | bytes 1048608 | tf_op jit(solution)/shard_map/ppermute | solution.py:72
  218.1 3.3 fusion.90
  244.3 6.8 %collective-permute-done.20 = bf16[128,1024]{1,0:T(8,128)(2,1)S(1)} collective-permute-done((bf16[128,1024]{1,0:T(8,128)(2,1)S(1)}, bf16[128,1024]{1,0:T(8,128)(2,1)S(1)}, u32[]{:S(2)}, u32[]{:S(2)}) %collective-permute-start.20) | collective-permute-done | bytes 262176 | tf_op jit(solution)/shard_map/ppermute | solution.py:16
  253.4 3.3 collective-permute-done.26
  258.4 3.9 collective-permute-done.21
  272.3 7.6 %collective-permute-done.35 = bf16[512,512]{1,0:T(8,128)(2,1)S(1)} collective-permute-done((bf16[512,512]{1,0:T(8,128)(2,1)S(1)}, bf16[512,512]{1,0:T(8,128)(2,1)S(1)}, u32[]{:S(2)}, u32[]{:S(2)}) %collective-permute-start.35) | collective-permute-done | bytes 524320 | tf_op jit(solution)/shard_map/ppermute | solution.py:76
  286.1 8.5 %collective-permute-done.38 = bf16[128,512]{1,0:T(8,128)(2,1)S(1)} collective-permute-done((bf16[128,512]{1,0:T(8,128)(2,1)S(1)}, bf16[128,512]{1,0:T(8,128)(2,1)S(1)}, u32[]{:S(2)}, u32[]{:S(2)}) %collective-permute-start.38) | collective-permute-done | bytes 131104 | tf_op jit(solution)/shard_map/ppermute | solution.py:16
  296.6 15.6 %collective-permute-done.41 = bf16[512,1536]{1,0:T(8,128)(2,1)S(1)} collective-permute-done((bf16[512,1536]{1,0:T(8,128)(2,1)S(1)}, bf16[512,1536]{1,0:T(8,128)(2,1)S(1)}, u32[]{:S(2)}, u32[]{:S(2)}) %collective-permute-start.41) | collective-permute-done | bytes 1572896 | tf_op jit(solution)/shard_map/ppermute | solution.py:72
  317.9 6.2 %collective-permute-done.39 = bf16[128,512]{1,0:T(8,128)(2,1)S(1)} collective-permute-done((bf16[128,512]{1,0:T(8,128)(2,1)S(1)}, bf16[128,512]{1,0:T(8,128)(2,1)S(1)}, u32[]{:S(2)}, u32[]{:S(2)}) %collective-permute-start.39) | collective-permute-done | bytes 131104 | tf_op jit(solution)/shard_map/ppermute | solution.py:16
  325.2 22.3 %collective-permute-done.42 = bf16[512,1536]{1,0:T(8,128)(2,1)S(1)} collective-permute-done((bf16[512,1536]{1,0:T(8,128)(2,1)S(1)}, bf16[512,1536]{1,0:T(8,128)(2,1)S(1)}, u32[]{:S(2)}, u32[]{:S(2)}) %collective-permute-start.42) | collective-permute-done | bytes 1572896 | tf_op jit(solution)/shard_map/ppermute | solution.py:72
  352.6 29.6 %collective-permute-done.43 = bf16[512,1536]{1,0:T(8,128)(2,1)S(1)} collective-permute-done((bf16[512,1536]{1,0:T(8,128)(2,1)S(1)}, bf16[512,1536]{1,0:T(8,128)(2,1)S(1)}, u32[]{:S(2)}, u32[]{:S(2)}) %collective-permute-start.43) | collective-permute-done | bytes 1572896 | tf_op jit(solution)/shard_map/ppermute | solution.py:72
  389.9 12.9 %collective-permute-done.44 = bf16[256,1536]{1,0:T(8,128)(2,1)S(1)} collective-permute-done((bf16[256,1536]{1,0:T(8,128)(2,1)S(1)}, bf16[256,1536]{1,0:T(8,128)(2,1)S(1)}, u32[]{:S(2)}, u32[]{:S(2)}) %collective-permute-start.44) | collective-permute-done | bytes 786464 | tf_op jit(solution)/shard_map/ppermute | solution.py:76
  420.2 3.4 fusion.227
  438.1 17.7 %collective-permute-done.55 = bf16[1024,512]{1,0:T(8,128)(2,1)S(1)} collective-permute-done((bf16[1024,512]{1,0:T(8,128)(2,1)}, bf16[1024,512]{1,0:T(8,128)(2,1)S(1)}, u32[]{:S(2)}, u32[]{:S(2)}) %collective-permute-start.55) | collective-permute-done | bytes 1048608 | tf_op jit(solution)/shard_map/ppermute | solution.py:72
  465.0 4.8 collective-permute-done.54
  470.1 4.2 collective-permute-done.58
  474.5 12.2 %collective-permute-done.59 = bf16[1024,512]{1,0:T(8,128)(2,1)S(1)} collective-permute-done((bf16[1024,512]{1,0:T(8,128)(2,1)S(1)}, bf16[1024,512]{1,0:T(8,128)(2,1)S(1)}, u32[]{:S(2)}, u32[]{:S(2)}) %collective-permute-start.59) | collective-permute-done | bytes 1048608 | tf_op jit(solution)/shard_map/ppermute | solution.py:72
  490.8 8.7 %collective-permute-done.63 = bf16[512,512]{1,0:T(8,128)(2,1)S(1)} collective-permute-done((bf16[512,512]{1,0:T(8,128)(2,1)S(1)}, bf16[512,512]{1,0:T(8,128)(2,1)S(1)}, u32[]{:S(2)}, u32[]{:S(2)}) %collective-permute-start.63) | collective-permute-done | bytes 524320 | tf_op jit(solution)/shard_map/ppermute | solution.py:76
  503.6 6.8 %collective-permute-done.62 = bf16[128,1024]{1,0:T(8,128)(2,1)S(1)} collective-permute-done((bf16[128,1024]{1,0:T(8,128)(2,1)S(1)}, bf16[128,1024]{1,0:T(8,128)(2,1)S(1)}, u32[]{:S(2)}, u32[]{:S(2)}) %collective-permute-start.62) | collective-permute-done | bytes 262176 | tf_op jit(solution)/shard_map/ppermute | solution.py:16
  (404 shorter events, 199.3 us)
Async XLA Ops:
  9.0 40.8 %collective-permute-start.1 = (bf16[512,1536]{1,0:T(8,128)(2,1)S(1)}, bf16[512,1536]{1,0:T(8,128)(2,1)}, u32[]{:S(2)}, u32[]{:S(2)}) collective-permute-start(bf16[512,1536]{1,0:T(8,128)(2,1)S(1)} %get-tuple-element.63), channel_id=1, source_target_pairs={{0,8},{8,16},{16,24},{24,28},{28,20},{20,12},{12,4},{4,0},{1,9},{9... | collective-permute-start | bytes 4718600 | tf_op jit(solution)/shard_map/ppermute | solution.py:72
  20.2 29.6 %all-to-all-start = ((s32[8,1,128]{2,1,0:T(1,128)}), s32[8,1,128]{2,1,0:T(1,128)S(1)}, u32[]{:S(2)}, u32[]{:S(2)}) async-start(s32[8,1,128]{2,1,0:T(1,128)} %bitcast.8), calls=%async_computation | async-start | bytes 8192 | tf_op jit(solution)/shard_map/all_to_all | solution.py:186
  29.0 40.9 %collective-permute-start.8 = (bf16[512,1536]{1,0:T(8,128)(2,1)S(1)}, bf16[512,1536]{1,0:T(8,128)(2,1)}, u32[]{:S(2)}, u32[]{:S(2)}) collective-permute-start(bf16[512,1536]{1,0:T(8,128)(2,1)S(1)} %get-tuple-element.63), channel_id=1, source_target_pairs={{8,0},{16,8},{24,16},{28,24},{20,28},{12,20},{4,12},{0,4},{9,1},{1... | collective-permute-start | bytes 4718600 | tf_op jit(solution)/shard_map/ppermute | solution.py:73
  49.7 40.6 %all-to-all-start.1 = ((bf16[8,64,1024]{2,1,0:T(8,128)(2,1)}), bf16[8,64,1024]{2,1,0:T(8,128)(2,1)S(1)}, u32[]{:S(2)}, u32[]{:S(2)}) async-start(bf16[8,64,1024]{2,1,0:T(8,128)(2,1)} %broadcast_select_fusion.4), calls=%async_computation.1 | async-start | bytes 2097152 | tf_op jit(solution)/shard_map/all_to_all | solution.py:190
  53.3 50.2 %collective-permute-start.5 = (bf16[512,1536]{1,0:T(8,128)(2,1)}, bf16[512,1536]{1,0:T(8,128)(2,1)}, u32[]{:S(2)}, u32[]{:S(2)}) collective-permute-start(bf16[512,1536]{1,0:T(8,128)(2,1)} %collective-permute-done.1), channel_id=1, source_target_pairs={{0,8},{8,16},{16,24},{24,28},{28,20},{20,12},{12,4},{4,0},{1,9},{9... | collective-permute-start | bytes 4718600 | tf_op jit(solution)/shard_map/ppermute | solution.py:72
  69.9 45.7 %collective-permute-start.9 = (bf16[512,1536]{1,0:T(8,128)(2,1)}, bf16[512,1536]{1,0:T(8,128)(2,1)}, u32[]{:S(2)}, u32[]{:S(2)}) collective-permute-start(bf16[512,1536]{1,0:T(8,128)(2,1)} %collective-permute-done.8), channel_id=1, source_target_pairs={{8,0},{16,8},{24,16},{28,24},{20,28},{12,20},{4,12},{0,4},{9,1},{1... | collective-permute-start | bytes 4718600 | tf_op jit(solution)/shard_map/ppermute | solution.py:73
  90.3 28.3 %collective-permute-start.2 = (bf16[512,1024]{1,0:T(8,128)(2,1)S(1)}, bf16[512,1024]{1,0:T(8,128)(2,1)}, u32[]{:S(2)}, u32[]{:S(2)}) collective-permute-start(bf16[512,1024]{1,0:T(8,128)(2,1)S(1)} %bitcast.143), channel_id=1, source_target_pairs={{0,1},{1,0},{2,3},{3,2},{4,5},{5,4},{6,7},{7,6},{8,9},{9,8},{10,11... | collective-permute-start | bytes 3145736 | tf_op jit(solution)/shard_map/ppermute | solution.py:16
  103.5 40.7 %collective-permute-start.6 = (bf16[512,1536]{1,0:T(8,128)(2,1)}, bf16[512,1536]{1,0:T(8,128)(2,1)S(1)}, u32[]{:S(2)}, u32[]{:S(2)}) collective-permute-start(bf16[512,1536]{1,0:T(8,128)(2,1)} %collective-permute-done.5), channel_id=1, source_target_pairs={{0,8},{8,16},{16,24},{24,28},{28,20},{20,12},{12,4},{4,0},{1,9},{9... | collective-permute-start | bytes 4718600 | tf_op jit(solution)/shard_map/ppermute | solution.py:72
  115.6 40.6 %collective-permute-start.10 = (bf16[512,1536]{1,0:T(8,128)(2,1)}, bf16[512,1536]{1,0:T(8,128)(2,1)}, u32[]{:S(2)}, u32[]{:S(2)}) collective-permute-start(bf16[512,1536]{1,0:T(8,128)(2,1)} %collective-permute-done.9), channel_id=1, source_target_pairs={{8,0},{16,8},{24,16},{28,24},{20,28},{12,20},{4,12},{0,4},{9,1},{1... | collective-permute-start | bytes 4718600 | tf_op jit(solution)/shard_map/ppermute | solution.py:73
  122.0 62.9 %collective-permute-start.3 = (bf16[512,2048]{1,0:T(8,128)(2,1)}, bf16[512,2048]{1,0:T(8,128)(2,1)}, u32[]{:S(2)}, u32[]{:S(2)}) collective-permute-start(bf16[512,2048]{1,0:T(8,128)(2,1)} %pad_maximum_fusion), channel_id=1, source_target_pairs={{0,2},{2,0},{1,3},{3,1},{4,6},{6,4},{5,7},{7,5},{8,10},{10,8},{9,1... | collective-permute-start | bytes 6291464 | tf_op jit(solution)/shard_map/ppermute | solution.py:16
  156.2 26.4 %collective-permute-start.17 = (bf16[1024,512]{1,0:T(8,128)(2,1)}, bf16[1024,512]{1,0:T(8,128)(2,1)}, u32[]{:S(2)}, u32[]{:S(2)}) collective-permute-start(bf16[1024,512]{1,0:T(8,128)(2,1)} %get-tuple-element.16), channel_id=1, source_target_pairs={{0,8},{8,16},{16,24},{24,28},{28,20},{20,12},{12,4},{4,0},{1,9},{9... | collective-permute-start | bytes 3145736 | tf_op jit(solution)/shard_map/ppermute | solution.py:72
  158.0 26.4 %collective-permute-start.18 = (bf16[1024,512]{1,0:T(8,128)(2,1)}, bf16[1024,512]{1,0:T(8,128)(2,1)}, u32[]{:S(2)}, u32[]{:S(2)}) collective-permute-start(bf16[1024,512]{1,0:T(8,128)(2,1)} %get-tuple-element.16), channel_id=1, source_target_pairs={{8,0},{16,8},{24,16},{28,24},{20,28},{12,20},{4,12},{0,4},{9,1},{1... | collective-permute-start | bytes 3145736 | tf_op jit(solution)/shard_map/ppermute | solution.py:73
  161.4 39.9 %collective-permute-start.7 = (bf16[256,1536]{1,0:T(8,128)(2,1)S(1)}, bf16[256,1536]{1,0:T(8,128)(2,1)S(1)}, u32[]{:S(2)}, u32[]{:S(2)}) collective-permute-start(bf16[256,1536]{1,0:T(8,128)(2,1)S(1)} %slice.355), channel_id=1, source_target_pairs={{0,8},{8,16},{16,24},{24,28},{28,20},{20,12},{12,4},{4,0},{1,9},{9... | collective-permute-start | bytes 2359304 | tf_op jit(solution)/shard_map/ppermute | solution.py:76
  164.4 36.9 %collective-permute-start.11 = (bf16[256,1536]{1,0:T(8,128)(2,1)S(1)}, bf16[256,1536]{1,0:T(8,128)(2,1)S(1)}, u32[]{:S(2)}, u32[]{:S(2)}) collective-permute-start(bf16[256,1536]{1,0:T(8,128)(2,1)S(1)} %slice.356), channel_id=1, source_target_pairs={{8,0},{16,8},{24,16},{28,24},{20,28},{12,20},{4,12},{0,4},{9,1},{1... | collective-permute-start | bytes 2359304 | tf_op jit(solution)/shard_map/ppermute | solution.py:77
  182.6 52.5 %collective-permute-start.23 = (bf16[1024,512]{1,0:T(8,128)(2,1)}, bf16[1024,512]{1,0:T(8,128)(2,1)}, u32[]{:S(2)}, u32[]{:S(2)}) collective-permute-start(bf16[1024,512]{1,0:T(8,128)(2,1)} %collective-permute-done.17), channel_id=1, source_target_pairs={{0,8},{8,16},{16,24},{24,28},{28,20},{20,12},{12,4},{4,0},{1,9},{9... | collective-permute-start | bytes 3145736 | tf_op jit(solution)/shard_map/ppermute | solution.py:72
  184.4 52.7 %collective-permute-start.24 = (bf16[1024,512]{1,0:T(8,128)(2,1)}, bf16[1024,512]{1,0:T(8,128)(2,1)}, u32[]{:S(2)}, u32[]{:S(2)}) collective-permute-start(bf16[1024,512]{1,0:T(8,128)(2,1)} %collective-permute-done.18), channel_id=1, source_target_pairs={{8,0},{16,8},{24,16},{28,24},{20,28},{12,20},{4,12},{0,4},{9,1},{1... | collective-permute-start | bytes 3145736 | tf_op jit(solution)/shard_map/ppermute | solution.py:73
  239.2 25.8 %collective-permute-start.29 = (bf16[1024,512]{1,0:T(8,128)(2,1)}, bf16[1024,512]{1,0:T(8,128)(2,1)S(1)}, u32[]{:S(2)}, u32[]{:S(2)}) collective-permute-start(bf16[1024,512]{1,0:T(8,128)(2,1)} %collective-permute-done.23), channel_id=1, source_target_pairs={{0,8},{8,16},{16,24},{24,28},{28,20},{20,12},{12,4},{4,0},{1,9},{9... | collective-permute-start | bytes 3145736 | tf_op jit(solution)/shard_map/ppermute | solution.py:72
  241.0 25.8 %collective-permute-start.30 = (bf16[1024,512]{1,0:T(8,128)(2,1)}, bf16[1024,512]{1,0:T(8,128)(2,1)S(1)}, u32[]{:S(2)}, u32[]{:S(2)}) collective-permute-start(bf16[1024,512]{1,0:T(8,128)(2,1)} %collective-permute-done.24), channel_id=1, source_target_pairs={{8,0},{16,8},{24,16},{28,24},{20,28},{12,20},{4,12},{0,4},{9,1},{1... | collective-permute-start | bytes 3145736 | tf_op jit(solution)/shard_map/ppermute | solution.py:73
  252.8 33.3 %collective-permute-start.14 = (bf16[128,512]{1,0:T(8,128)(2,1)S(1)}, bf16[128,512]{1,0:T(8,128)(2,1)S(1)}, u32[]{:S(2)}, u32[]{:S(2)}) collective-permute-start(bf16[128,512]{1,0:T(8,128)(2,1)S(1)} %select_convert_fusion.19), channel_id=1, source_target_pairs={{0,1},{1,0},{2,3},{3,2},{4,5},{5,4},{6,7},{7,6},{8,9},{9,8},{10,11... | collective-permute-start | bytes 393224 | tf_op jit(solution)/shard_map/ppermute | solution.py:16
  270.0 42.2 %collective-permute-start.41 = (bf16[512,1536]{1,0:T(8,128)(2,1)S(1)}, bf16[512,1536]{1,0:T(8,128)(2,1)S(1)}, u32[]{:S(2)}, u32[]{:S(2)}) collective-permute-start(bf16[512,1536]{1,0:T(8,128)(2,1)S(1)} %copy-done.22), channel_id=1, source_target_pairs={{0,8},{8,16},{16,24},{24,28},{28,20},{20,12},{12,4},{4,0},{1,9},{9... | collective-permute-start | bytes 4718600 | tf_op jit(solution)/shard_map/ppermute | solution.py:72
  279.9 34.1 %collective-permute-start.45 = (bf16[512,1536]{1,0:T(8,128)(2,1)S(1)}, bf16[512,1536]{1,0:T(8,128)(2,1)S(1)}, u32[]{:S(2)}, u32[]{:S(2)}) collective-permute-start(bf16[512,1536]{1,0:T(8,128)(2,1)S(1)} %copy-done.22), channel_id=1, source_target_pairs={{8,0},{16,8},{24,16},{28,24},{20,28},{12,20},{4,12},{0,4},{9,1},{1... | collective-permute-start | bytes 4718600 | tf_op jit(solution)/shard_map/ppermute | solution.py:73
  283.2 32.3 %collective-permute-start.32 = (bf16[128,1024]{1,0:T(8,128)(2,1)S(1)}, bf16[128,1024]{1,0:T(8,128)(2,1)S(1)}, u32[]{:S(2)}, u32[]{:S(2)}) collective-permute-start(bf16[128,1024]{1,0:T(8,128)(2,1)S(1)} %select_convert_fusion.12), channel_id=1, source_target_pairs={{0,1},{1,0},{2,3},{3,2},{4,5},{5,4},{6,7},{7,6},{8,9},{9,8},{10,11... | collective-permute-start | bytes 786440 | tf_op jit(solution)/shard_map/ppermute | solution.py:16
  312.3 35.2 %collective-permute-start.42 = (bf16[512,1536]{1,0:T(8,128)(2,1)S(1)}, bf16[512,1536]{1,0:T(8,128)(2,1)S(1)}, u32[]{:S(2)}, u32[]{:S(2)}) collective-permute-start(bf16[512,1536]{1,0:T(8,128)(2,1)S(1)} %collective-permute-done.41), channel_id=1, source_target_pairs={{0,8},{8,16},{16,24},{24,28},{28,20},{20,12},{12,4},{4,0},{1,9},{9... | collective-permute-start | bytes 4718600 | tf_op jit(solution)/shard_map/ppermute | solution.py:72
  314.0 35.1 %collective-permute-start.46 = (bf16[512,1536]{1,0:T(8,128)(2,1)S(1)}, bf16[512,1536]{1,0:T(8,128)(2,1)S(1)}, u32[]{:S(2)}, u32[]{:S(2)}) collective-permute-start(bf16[512,1536]{1,0:T(8,128)(2,1)S(1)} %collective-permute-done.45), channel_id=1, source_target_pairs={{8,0},{16,8},{24,16},{28,24},{20,28},{12,20},{4,12},{0,4},{9,1},{1... | collective-permute-start | bytes 4718600 | tf_op jit(solution)/shard_map/ppermute | solution.py:73
  324.1 25.4 %collective-permute-start.40 = (bf16[256,512]{1,0:T(8,128)(2,1)S(1)}, bf16[256,512]{1,0:T(8,128)(2,1)S(1)}, u32[]{:S(2)}, u32[]{:S(2)}) collective-permute-start(bf16[256,512]{1,0:T(8,128)(2,1)S(1)} %pad_maximum_fusion.19), channel_id=1, source_target_pairs={{0,2},{2,0},{1,3},{3,1},{4,6},{6,4},{5,7},{7,5},{8,10},{10,8},{9,1... | collective-permute-start | bytes 786440 | tf_op jit(solution)/shard_map/ppermute | solution.py:16
  324.3 25.5 %collective-permute-start.34 = (bf16[256,1024]{1,0:T(8,128)(2,1)S(1)}, bf16[256,1024]{1,0:T(8,128)(2,1)S(1)}, u32[]{:S(2)}, u32[]{:S(2)}) collective-permute-start(bf16[256,1024]{1,0:T(8,128)(2,1)S(1)} %pad_maximum_fusion.13), channel_id=1, source_target_pairs={{0,2},{2,0},{1,3},{3,1},{4,6},{6,4},{5,7},{7,5},{8,10},{10,8},{9,1... | collective-permute-start | bytes 1572872 | tf_op jit(solution)/shard_map/ppermute | solution.py:16
  347.5 34.7 %collective-permute-start.43 = (bf16[512,1536]{1,0:T(8,128)(2,1)S(1)}, bf16[512,1536]{1,0:T(8,128)(2,1)S(1)}, u32[]{:S(2)}, u32[]{:S(2)}) collective-permute-start(bf16[512,1536]{1,0:T(8,128)(2,1)S(1)} %collective-permute-done.42), channel_id=1, source_target_pairs={{0,8},{8,16},{16,24},{24,28},{28,20},{20,12},{12,4},{4,0},{1,9},{9... | collective-permute-start | bytes 4718600 | tf_op jit(solution)/shard_map/ppermute | solution.py:72
  349.1 34.6 %collective-permute-start.47 = (bf16[512,1536]{1,0:T(8,128)(2,1)S(1)}, bf16[512,1536]{1,0:T(8,128)(2,1)S(1)}, u32[]{:S(2)}, u32[]{:S(2)}) collective-permute-start(bf16[512,1536]{1,0:T(8,128)(2,1)S(1)} %collective-permute-done.46), channel_id=1, source_target_pairs={{8,0},{16,8},{24,16},{28,24},{20,28},{12,20},{4,12},{0,4},{9,1},{1... | collective-permute-start | bytes 4718600 | tf_op jit(solution)/shard_map/ppermute | solution.py:73
  387.6 42.4 %collective-permute-start.51 = (bf16[1024,512]{1,0:T(8,128)(2,1)}, bf16[1024,512]{1,0:T(8,128)(2,1)}, u32[]{:S(2)}, u32[]{:S(2)}) collective-permute-start(bf16[1024,512]{1,0:T(8,128)(2,1)} %get-tuple-element.19), channel_id=1, source_target_pairs={{0,8},{8,16},{16,24},{24,28},{28,20},{20,12},{12,4},{4,0},{1,9},{9... | collective-permute-start | bytes 3145736 | tf_op jit(solution)/shard_map/ppermute | solution.py:72
  389.0 43.7 %collective-permute-start.52 = (bf16[1024,512]{1,0:T(8,128)(2,1)}, bf16[1024,512]{1,0:T(8,128)(2,1)}, u32[]{:S(2)}, u32[]{:S(2)}) collective-permute-start(bf16[1024,512]{1,0:T(8,128)(2,1)} %get-tuple-element.19), channel_id=1, source_target_pairs={{8,0},{16,8},{24,16},{28,24},{20,28},{12,20},{4,12},{0,4},{9,1},{1... | collective-permute-start | bytes 3145736 | tf_op jit(solution)/shard_map/ppermute | solution.py:73
  430.0 25.8 %collective-permute-start.55 = (bf16[1024,512]{1,0:T(8,128)(2,1)}, bf16[1024,512]{1,0:T(8,128)(2,1)S(1)}, u32[]{:S(2)}, u32[]{:S(2)}) collective-permute-start(bf16[1024,512]{1,0:T(8,128)(2,1)} %collective-permute-done.51), channel_id=1, source_target_pairs={{0,8},{8,16},{16,24},{24,28},{28,20},{20,12},{12,4},{4,0},{1,9},{9... | collective-permute-start | bytes 3145736 | tf_op jit(solution)/shard_map/ppermute | solution.py:72
  432.8 25.5 %collective-permute-start.56 = (bf16[1024,512]{1,0:T(8,128)(2,1)}, bf16[1024,512]{1,0:T(8,128)(2,1)S(1)}, u32[]{:S(2)}, u32[]{:S(2)}) collective-permute-start(bf16[1024,512]{1,0:T(8,128)(2,1)} %collective-permute-done.52), channel_id=1, source_target_pairs={{8,0},{16,8},{24,16},{28,24},{20,28},{12,20},{4,12},{0,4},{9,1},{1... | collective-permute-start | bytes 3145736 | tf_op jit(solution)/shard_map/ppermute | solution.py:73
  (100 other events, 1420.3 us)

commit v4 on v3

--- a/solution.py
+++ b/solution.py
@@ -58,7 +58,7 @@
     ]
 
 
-def ring_gather(own, before):
+def ring_gather(own, before, release):
     count = lax.axis_size("dp")
     order = ring_order(count)
     right = [(order[i], order[(i + 1) % count]) for i in range(count)]
@@ -76,7 +76,7 @@
     top = lax.ppermute(onward[:half], "dp", right)
     low = lax.ppermute(back[half:], "dp", left)
     parts[count // 2] = jnp.concatenate([top, low], axis=0)
-    return parts, (onward, back)
+    return parts, (parts[release], parts[count - release])
 
 
 def turn_factors(places):
@@ -156,7 +156,7 @@
     joined = both_layers((w_query[0], w_key[0], w_value[0]), 1, (True, split, split))
     query_width = w_query.shape[2] // phases
     key_width = w_key.shape[2] // (phases if split else 1)
-    first_ring = ring_gather(joined[0], None)
+    first_ring = ring_gather(joined[0], None, replicas // 2 - 1)
     out_parts = both_layers((w_out[0],), 0, (True,))
     first = section == 0
     other_gain = swapped(norm_gain[0], "section")
@@ -200,8 +200,8 @@
     states = [lax.dynamic_slice_in_dim(packed, s, chunk, 1) for s in starts]
     before = None
     for level in range(phases):
-        projections, before = ring_gather(joined[level], before) if level else first_ring
-        outs, before = ring_gather(out_parts[level], before)
+        projections, before = ring_gather(joined[level], before, replicas // 2 - 2) if level else first_ring
+        outs, before = ring_gather(out_parts[level], before, 1)
         total = sum(
             jnp.sum(jnp.square(piece.astype(F32)), axis=-1, keepdims=True) for piece in states
         )

time: 521 us -> 543 us (1.042)
  waiting for transfers between devices: 298 us -> 311 us
  matrix products: 56.4 us -> 62.7 us
    ppermute x12, waiting for transfers between devices: 33.3 us -> 67.1 us  [ring_gather(): back = lax.ppermute(back, 'dp', left)]
    ppermute x12, waiting for transfers between devices: 144 us -> 127 us  [ring_gather(): onward = lax.ppermute(onward, 'dp', right)]
    ppermute x4, waiting for transfers between devices: 29.2 us -> 16.9 us  [ring_gather(): top = lax.ppermute(onward[:half], 'dp', right)]
    ppermute x4, waiting for transfers between devices: 2.01 us -> 12 us  [ring_gather(): low = lax.ppermute(back[half:], 'dp', left)]
    ppermute x12, starting transfers between devices: 25.2 us -> 17.8 us  [ring_gather(): onward = lax.ppermute(onward, 'dp', right)]
    unnamed x130 -> x142, local copies, waits for them, and re-layouts: 10.9 us -> 10.2 us
  transfers between devices with their start and end apart: 69 -> 69, of which waited for: 34 -> 37; matrix products, arithmetic and copies ran while one was open for 25% -> 26% of each run, Pallas kernels for 0% -> 0%
where the time goes in v4:
time: 543 us; the launch traced here: 536 us
  waiting for transfers between devices  311 us (57%)
  starting transfers between devices  76.4 us (14%)
  matrix products  62.7 us (12%)
  local copies, waits for them, and re-layouts  45.3 us (8%)
  other arithmetic  39.1 us (7%)
    ppermute x12, waiting for transfers between devices, ring_gather(): onward = lax.ppermute(onward, 'dp', right)  127 us
    ppermute x12, waiting for transfers between devices, ring_gather(): back = lax.ppermute(back, 'dp', left)  67.1 us
    ppermute x35, waiting for transfers between devices, swapped(): return lax.ppermute(array, axis, [(0, 1), (1, 0)])  54 us
    dot_general x16, matrix products, per_device(): projected += jnp.dot(normed, projections[k], preferred_element_type=F32)  27.4 us
    ppermute x35, starting transfers between devices, swapped(): return lax.ppermute(array, axis, [(0, 1), (1, 0)])  24.7 us
    dot_general x16, matrix products, per_device(): jnp.dot(mixed_heads, outs[k], preferred_element_type=F32)  24.1 us
    ppermute x12, starting transfers between devices, ring_gather(): onward = lax.ppermute(onward, 'dp', right)  17.8 us
    all_to_all x1, waiting for transfers between devices, per_device(): lax.all_to_all(send_rows, 'dp', split_axis=0, concat_axis=0, tiled=True)  17.6 us
  transfers between devices with their start and end apart: 69, of which 37 were waited for; matrix products, arithmetic and copies ran while one was open for 26% of the time, Pallas kernels for 0%

profile of v4, /device:TPU:0, one launch (start us, length us, event | category | flops | bytes accessed | tf_op | source)
XLA Modules:
  0.0 536.2 jit_solution(16617141330909924369)
XLA Ops:
  12.2 3.5 gather_fusion.1
  15.8 3.5 gather_fusion.2
  20.2 4.8 all-to-all-start
  33.5 16.3 %all-to-all-done = s32[8,1,128]{2,1,0:T(1,128)S(1)} async-done(((s32[8,1,128]{2,1,0:T(1,128)}), s32[8,1,128]{2,1,0:T(1,128)S(1)}, u32[]{:S(2)}, u32[]{:S(2)}) %all-to-all-start) | async-done | bytes 4128 | tf_op jit(solution)/shard_map/all_to_all | solution.py:186
  49.8 3.6 all-to-all-start.1
  55.2 14.6 %collective-permute-done.8 = bf16[512,1536]{1,0:T(8,128)(2,1)} collective-permute-done((bf16[512,1536]{1,0:T(8,128)(2,1)S(1)}, bf16[512,1536]{1,0:T(8,128)(2,1)}, u32[]{:S(2)}, u32[]{:S(2)}) %collective-permute-start.8) | collective-permute-done | bytes 1572896 | tf_op jit(solution)/shard_map/ppermute | solution.py:73
  72.7 17.6 %all-to-all-done.1 = bf16[8,64,1024]{2,1,0:T(8,128)(2,1)S(1)} async-done(((bf16[8,64,1024]{2,1,0:T(8,128)(2,1)}), bf16[8,64,1024]{2,1,0:T(8,128)(2,1)S(1)}, u32[]{:S(2)}, u32[]{:S(2)}) %all-to-all-start.1) | async-done | bytes 1048608 | tf_op jit(solution)/shard_map/all_to_all | solution.py:190
  91.9 11.7 %collective-permute-done.5 = bf16[512,1536]{1,0:T(8,128)(2,1)} collective-permute-done((bf16[512,1536]{1,0:T(8,128)(2,1)}, bf16[512,1536]{1,0:T(8,128)(2,1)}, u32[]{:S(2)}, u32[]{:S(2)}) %collective-permute-start.5) | collective-permute-done | bytes 1572896 | tf_op jit(solution)/shard_map/ppermute | solution.py:72
  103.5 7.1 %collective-permute-start.6 = (bf16[512,1536]{1,0:T(8,128)(2,1)}, bf16[512,1536]{1,0:T(8,128)(2,1)S(1)}, u32[]{:S(2)}, u32[]{:S(2)}) collective-permute-start(bf16[512,1536]{1,0:T(8,128)(2,1)} %collective-permute-done.5), channel_id=1, source_target_pairs={{0,8},{8,16},{16,24},{24,28},{28,20},{20,12},{12,4},{4,0},{1,9},{9... | collective-permute-start | bytes 4718600 | tf_op jit(solution)/shard_map/ppermute | solution.py:72
  110.7 4.9 collective-permute-done.9
  122.8 3.4 collective-permute-done.4
  126.2 3.3 bitcast_select_fusion.8
  129.5 14.8 %collective-permute-done.6 = bf16[512,1536]{1,0:T(8,128)(2,1)S(1)} collective-permute-done((bf16[512,1536]{1,0:T(8,128)(2,1)}, bf16[512,1536]{1,0:T(8,128)(2,1)S(1)}, u32[]{:S(2)}, u32[]{:S(2)}) %collective-permute-start.6) | collective-permute-done | bytes 1572896 | tf_op jit(solution)/shard_map/ppermute | solution.py:72
  144.3 11.9 %collective-permute-done.10 = bf16[512,1536]{1,0:T(8,128)(2,1)} collective-permute-done((bf16[512,1536]{1,0:T(8,128)(2,1)}, bf16[512,1536]{1,0:T(8,128)(2,1)}, u32[]{:S(2)}, u32[]{:S(2)}) %collective-permute-start.10) | collective-permute-done | bytes 1572896 | tf_op jit(solution)/shard_map/ppermute | solution.py:73
  164.7 17.9 %collective-permute-done.17 = bf16[1024,512]{1,0:T(8,128)(2,1)} collective-permute-done((bf16[1024,512]{1,0:T(8,128)(2,1)}, bf16[1024,512]{1,0:T(8,128)(2,1)}, u32[]{:S(2)}, u32[]{:S(2)}) %collective-permute-start.17) | collective-permute-done | bytes 1048608 | tf_op jit(solution)/shard_map/ppermute | solution.py:72
  219.8 3.3 fusion.90
  236.8 15.5 %collective-permute-done.23 = bf16[1024,512]{1,0:T(8,128)(2,1)} collective-permute-done((bf16[1024,512]{1,0:T(8,128)(2,1)}, bf16[1024,512]{1,0:T(8,128)(2,1)}, u32[]{:S(2)}, u32[]{:S(2)}) %collective-permute-start.23) | collective-permute-done | bytes 1048608 | tf_op jit(solution)/shard_map/ppermute | solution.py:72
  261.5 6.8 %collective-permute-done.20 = bf16[128,1024]{1,0:T(8,128)(2,1)S(1)} collective-permute-done((bf16[128,1024]{1,0:T(8,128)(2,1)S(1)}, bf16[128,1024]{1,0:T(8,128)(2,1)S(1)}, u32[]{:S(2)}, u32[]{:S(2)}) %collective-permute-start.20) | collective-permute-done | bytes 262176 | tf_op jit(solution)/shard_map/ppermute | solution.py:16
  270.0 3.9 collective-permute-done.26
  274.7 3.7 collective-permute-done.21
  289.5 28.4 %collective-permute-done.45 = bf16[512,1536]{1,0:T(8,128)(2,1)S(1)} collective-permute-done((bf16[512,1536]{1,0:T(8,128)(2,1)}, bf16[512,1536]{1,0:T(8,128)(2,1)S(1)}, u32[]{:S(2)}, u32[]{:S(2)}) %collective-permute-start.45) | collective-permute-done | bytes 1572896 | tf_op jit(solution)/shard_map/ppermute | solution.py:73
  319.9 9.2 %collective-permute-done.36 = bf16[512,512]{1,0:T(8,128)(2,1)S(1)} collective-permute-done((bf16[512,512]{1,0:T(8,128)(2,1)S(1)}, bf16[512,512]{1,0:T(8,128)(2,1)S(1)}, u32[]{:S(2)}, u32[]{:S(2)}) %collective-permute-start.36) | collective-permute-done | bytes 524320 | tf_op jit(solution)/shard_map/ppermute | solution.py:77
  334.5 8.5 %collective-permute-done.38 = bf16[128,512]{1,0:T(8,128)(2,1)S(1)} collective-permute-done((bf16[128,512]{1,0:T(8,128)(2,1)S(1)}, bf16[128,512]{1,0:T(8,128)(2,1)S(1)}, u32[]{:S(2)}, u32[]{:S(2)}) %collective-permute-start.38) | collective-permute-done | bytes 131104 | tf_op jit(solution)/shard_map/ppermute | solution.py:16
  350.0 6.9 %collective-permute-done.39 = bf16[128,512]{1,0:T(8,128)(2,1)S(1)} collective-permute-done((bf16[128,512]{1,0:T(8,128)(2,1)S(1)}, bf16[128,512]{1,0:T(8,128)(2,1)S(1)}, u32[]{:S(2)}, u32[]{:S(2)}) %collective-permute-start.39) | collective-permute-done | bytes 131104 | tf_op jit(solution)/shard_map/ppermute | solution.py:16
  357.7 4.3 collective-permute-done.46
  372.3 15.8 %collective-permute-done.51 = bf16[1024,512]{1,0:T(8,128)(2,1)S(1)} collective-permute-done((bf16[1024,512]{1,0:T(8,128)(2,1)S(1)}, bf16[1024,512]{1,0:T(8,128)(2,1)S(1)}, u32[]{:S(2)}, u32[]{:S(2)}) %collective-permute-start.51) | collective-permute-done | bytes 1048608 | tf_op jit(solution)/shard_map/ppermute | solution.py:72
  390.2 31.7 %collective-permute-done.43 = bf16[512,1536]{1,0:T(8,128)(2,1)S(1)} collective-permute-done((bf16[512,1536]{1,0:T(8,128)(2,1)S(1)}, bf16[512,1536]{1,0:T(8,128)(2,1)S(1)}, u32[]{:S(2)}, u32[]{:S(2)}) %collective-permute-start.43) | collective-permute-done | bytes 1572896 | tf_op jit(solution)/shard_map/ppermute | solution.py:72
  427.4 17.1 %collective-permute-done.55 = bf16[1024,512]{1,0:T(8,128)(2,1)} collective-permute-done((bf16[1024,512]{1,0:T(8,128)(2,1)S(1)}, bf16[1024,512]{1,0:T(8,128)(2,1)}, u32[]{:S(2)}, u32[]{:S(2)}) %collective-permute-start.55) | collective-permute-done | bytes 1048608 | tf_op jit(solution)/shard_map/ppermute | solution.py:72
  446.6 14.6 %collective-permute-done.44 = bf16[256,1536]{1,0:T(8,128)(2,1)S(1)} collective-permute-done((bf16[256,1536]{1,0:T(8,128)(2,1)S(1)}, bf16[256,1536]{1,0:T(8,128)(2,1)S(1)}, u32[]{:S(2)}, u32[]{:S(2)}) %collective-permute-start.44) | collective-permute-done | bytes 786464 | tf_op jit(solution)/shard_map/ppermute | solution.py:76
  477.4 3.5 fusion.227
  481.0 3.6 fusion.33
  525.6 6.2 %collective-permute-done.62 = bf16[128,1024]{1,0:T(8,128)(2,1)S(1)} collective-permute-done((bf16[128,1024]{1,0:T(8,128)(2,1)S(1)}, bf16[128,1024]{1,0:T(8,128)(2,1)S(1)}, u32[]{:S(2)}, u32[]{:S(2)}) %collective-permute-start.62) | collective-permute-done | bytes 262176 | tf_op jit(solution)/shard_map/ppermute | solution.py:16
  (416 shorter events, 212.2 us)
Async XLA Ops:
  9.0 40.8 %collective-permute-start.1 = (bf16[512,1536]{1,0:T(8,128)(2,1)S(1)}, bf16[512,1536]{1,0:T(8,128)(2,1)}, u32[]{:S(2)}, u32[]{:S(2)}) collective-permute-start(bf16[512,1536]{1,0:T(8,128)(2,1)S(1)} %get-tuple-element.63), channel_id=1, source_target_pairs={{0,8},{8,16},{16,24},{24,28},{28,20},{20,12},{12,4},{4,0},{1,9},{9... | collective-permute-start | bytes 4718600 | tf_op jit(solution)/shard_map/ppermute | solution.py:72
  20.2 29.6 %all-to-all-start = ((s32[8,1,128]{2,1,0:T(1,128)}), s32[8,1,128]{2,1,0:T(1,128)S(1)}, u32[]{:S(2)}, u32[]{:S(2)}) async-start(s32[8,1,128]{2,1,0:T(1,128)} %bitcast.8), calls=%async_computation | async-start | bytes 8192 | tf_op jit(solution)/shard_map/all_to_all | solution.py:186
  29.0 40.9 %collective-permute-start.8 = (bf16[512,1536]{1,0:T(8,128)(2,1)S(1)}, bf16[512,1536]{1,0:T(8,128)(2,1)}, u32[]{:S(2)}, u32[]{:S(2)}) collective-permute-start(bf16[512,1536]{1,0:T(8,128)(2,1)S(1)} %get-tuple-element.63), channel_id=1, source_target_pairs={{8,0},{16,8},{24,16},{28,24},{20,28},{12,20},{4,12},{0,4},{9,1},{1... | collective-permute-start | bytes 4718600 | tf_op jit(solution)/shard_map/ppermute | solution.py:73
  49.8 40.6 %all-to-all-start.1 = ((bf16[8,64,1024]{2,1,0:T(8,128)(2,1)}), bf16[8,64,1024]{2,1,0:T(8,128)(2,1)S(1)}, u32[]{:S(2)}, u32[]{:S(2)}) async-start(bf16[8,64,1024]{2,1,0:T(8,128)(2,1)} %broadcast_select_fusion.4), calls=%async_computation.1 | async-start | bytes 2097152 | tf_op jit(solution)/shard_map/all_to_all | solution.py:190
  53.3 50.2 %collective-permute-start.5 = (bf16[512,1536]{1,0:T(8,128)(2,1)}, bf16[512,1536]{1,0:T(8,128)(2,1)}, u32[]{:S(2)}, u32[]{:S(2)}) collective-permute-start(bf16[512,1536]{1,0:T(8,128)(2,1)} %collective-permute-done.1), channel_id=1, source_target_pairs={{0,8},{8,16},{16,24},{24,28},{28,20},{20,12},{12,4},{4,0},{1,9},{9... | collective-permute-start | bytes 4718600 | tf_op jit(solution)/shard_map/ppermute | solution.py:72
  69.9 45.7 %collective-permute-start.9 = (bf16[512,1536]{1,0:T(8,128)(2,1)}, bf16[512,1536]{1,0:T(8,128)(2,1)}, u32[]{:S(2)}, u32[]{:S(2)}) collective-permute-start(bf16[512,1536]{1,0:T(8,128)(2,1)} %collective-permute-done.8), channel_id=1, source_target_pairs={{8,0},{16,8},{24,16},{28,24},{20,28},{12,20},{4,12},{0,4},{9,1},{1... | collective-permute-start | bytes 4718600 | tf_op jit(solution)/shard_map/ppermute | solution.py:73
  90.3 28.3 %collective-permute-start.2 = (bf16[512,1024]{1,0:T(8,128)(2,1)S(1)}, bf16[512,1024]{1,0:T(8,128)(2,1)}, u32[]{:S(2)}, u32[]{:S(2)}) collective-permute-start(bf16[512,1024]{1,0:T(8,128)(2,1)S(1)} %bitcast.143), channel_id=1, source_target_pairs={{0,1},{1,0},{2,3},{3,2},{4,5},{5,4},{6,7},{7,6},{8,9},{9,8},{10,11... | collective-permute-start | bytes 3145736 | tf_op jit(solution)/shard_map/ppermute | solution.py:16
  103.5 40.7 %collective-permute-start.6 = (bf16[512,1536]{1,0:T(8,128)(2,1)}, bf16[512,1536]{1,0:T(8,128)(2,1)S(1)}, u32[]{:S(2)}, u32[]{:S(2)}) collective-permute-start(bf16[512,1536]{1,0:T(8,128)(2,1)} %collective-permute-done.5), channel_id=1, source_target_pairs={{0,8},{8,16},{16,24},{24,28},{28,20},{20,12},{12,4},{4,0},{1,9},{9... | collective-permute-start | bytes 4718600 | tf_op jit(solution)/shard_map/ppermute | solution.py:72
  115.6 40.6 %collective-permute-start.10 = (bf16[512,1536]{1,0:T(8,128)(2,1)}, bf16[512,1536]{1,0:T(8,128)(2,1)}, u32[]{:S(2)}, u32[]{:S(2)}) collective-permute-start(bf16[512,1536]{1,0:T(8,128)(2,1)} %collective-permute-done.9), channel_id=1, source_target_pairs={{8,0},{16,8},{24,16},{28,24},{20,28},{12,20},{4,12},{0,4},{9,1},{1... | collective-permute-start | bytes 4718600 | tf_op jit(solution)/shard_map/ppermute | solution.py:73
  122.0 63.5 %collective-permute-start.3 = (bf16[512,2048]{1,0:T(8,128)(2,1)}, bf16[512,2048]{1,0:T(8,128)(2,1)}, u32[]{:S(2)}, u32[]{:S(2)}) collective-permute-start(bf16[512,2048]{1,0:T(8,128)(2,1)} %pad_maximum_fusion), channel_id=1, source_target_pairs={{0,2},{2,0},{1,3},{3,1},{4,6},{6,4},{5,7},{7,5},{8,10},{10,8},{9,1... | collective-permute-start | bytes 6291464 | tf_op jit(solution)/shard_map/ppermute | solution.py:16
  156.2 26.4 %collective-permute-start.17 = (bf16[1024,512]{1,0:T(8,128)(2,1)}, bf16[1024,512]{1,0:T(8,128)(2,1)}, u32[]{:S(2)}, u32[]{:S(2)}) collective-permute-start(bf16[1024,512]{1,0:T(8,128)(2,1)} %get-tuple-element.16), channel_id=1, source_target_pairs={{0,8},{8,16},{16,24},{24,28},{28,20},{20,12},{12,4},{4,0},{1,9},{9... | collective-permute-start | bytes 3145736 | tf_op jit(solution)/shard_map/ppermute | solution.py:72
  158.0 26.4 %collective-permute-start.18 = (bf16[1024,512]{1,0:T(8,128)(2,1)}, bf16[1024,512]{1,0:T(8,128)(2,1)}, u32[]{:S(2)}, u32[]{:S(2)}) collective-permute-start(bf16[1024,512]{1,0:T(8,128)(2,1)} %get-tuple-element.16), channel_id=1, source_target_pairs={{8,0},{16,8},{24,16},{28,24},{20,28},{12,20},{4,12},{0,4},{9,1},{1... | collective-permute-start | bytes 3145736 | tf_op jit(solution)/shard_map/ppermute | solution.py:73
  161.4 41.7 %collective-permute-start.7 = (bf16[256,1536]{1,0:T(8,128)(2,1)S(1)}, bf16[256,1536]{1,0:T(8,128)(2,1)S(1)}, u32[]{:S(2)}, u32[]{:S(2)}) collective-permute-start(bf16[256,1536]{1,0:T(8,128)(2,1)S(1)} %slice.355), channel_id=1, source_target_pairs={{0,8},{8,16},{16,24},{24,28},{28,20},{20,12},{12,4},{4,0},{1,9},{9... | collective-permute-start | bytes 2359304 | tf_op jit(solution)/shard_map/ppermute | solution.py:76
  164.4 38.7 %collective-permute-start.11 = (bf16[256,1536]{1,0:T(8,128)(2,1)S(1)}, bf16[256,1536]{1,0:T(8,128)(2,1)S(1)}, u32[]{:S(2)}, u32[]{:S(2)}) collective-permute-start(bf16[256,1536]{1,0:T(8,128)(2,1)S(1)} %slice.356), channel_id=1, source_target_pairs={{8,0},{16,8},{24,16},{28,24},{20,28},{12,20},{4,12},{0,4},{9,1},{1... | collective-permute-start | bytes 2359304 | tf_op jit(solution)/shard_map/ppermute | solution.py:77
  184.4 103.6 %collective-permute-start.41 = (bf16[512,1536]{1,0:T(8,128)(2,1)}, bf16[512,1536]{1,0:T(8,128)(2,1)}, u32[]{:S(2)}, u32[]{:S(2)}) collective-permute-start(bf16[512,1536]{1,0:T(8,128)(2,1)} %get-tuple-element.17), channel_id=1, source_target_pairs={{0,8},{8,16},{16,24},{24,28},{28,20},{20,12},{12,4},{4,0},{1,9},{9... | collective-permute-start | bytes 4718600 | tf_op jit(solution)/shard_map/ppermute | solution.py:72
  184.4 68.0 %collective-permute-start.23 = (bf16[1024,512]{1,0:T(8,128)(2,1)}, bf16[1024,512]{1,0:T(8,128)(2,1)}, u32[]{:S(2)}, u32[]{:S(2)}) collective-permute-start(bf16[1024,512]{1,0:T(8,128)(2,1)} %collective-permute-done.17), channel_id=1, source_target_pairs={{0,8},{8,16},{16,24},{24,28},{28,20},{20,12},{12,4},{4,0},{1,9},{9... | collective-permute-start | bytes 3145736 | tf_op jit(solution)/shard_map/ppermute | solution.py:72
  185.6 68.7 %collective-permute-start.24 = (bf16[1024,512]{1,0:T(8,128)(2,1)}, bf16[1024,512]{1,0:T(8,128)(2,1)}, u32[]{:S(2)}, u32[]{:S(2)}) collective-permute-start(bf16[1024,512]{1,0:T(8,128)(2,1)} %collective-permute-done.18), channel_id=1, source_target_pairs={{8,0},{16,8},{24,16},{28,24},{20,28},{12,20},{4,12},{0,4},{9,1},{1... | collective-permute-start | bytes 3145736 | tf_op jit(solution)/shard_map/ppermute | solution.py:73
  273.9 44.0 %collective-permute-start.45 = (bf16[512,1536]{1,0:T(8,128)(2,1)}, bf16[512,1536]{1,0:T(8,128)(2,1)S(1)}, u32[]{:S(2)}, u32[]{:S(2)}) collective-permute-start(bf16[512,1536]{1,0:T(8,128)(2,1)} %get-tuple-element.17), channel_id=1, source_target_pairs={{8,0},{16,8},{24,16},{28,24},{20,28},{12,20},{4,12},{0,4},{9,1},{1... | collective-permute-start | bytes 4718600 | tf_op jit(solution)/shard_map/ppermute | solution.py:73
  284.2 34.0 %collective-permute-start.35 = (bf16[512,512]{1,0:T(8,128)(2,1)S(1)}, bf16[512,512]{1,0:T(8,128)(2,1)S(1)}, u32[]{:S(2)}, u32[]{:S(2)}) collective-permute-start(bf16[512,512]{1,0:T(8,128)(2,1)S(1)} %slice.386), channel_id=1, source_target_pairs={{0,8},{8,16},{16,24},{24,28},{28,20},{20,12},{12,4},{4,0},{1,9},{9... | collective-permute-start | bytes 1572872 | tf_op jit(solution)/shard_map/ppermute | solution.py:76
  285.7 43.5 %collective-permute-start.36 = (bf16[512,512]{1,0:T(8,128)(2,1)S(1)}, bf16[512,512]{1,0:T(8,128)(2,1)S(1)}, u32[]{:S(2)}, u32[]{:S(2)}) collective-permute-start(bf16[512,512]{1,0:T(8,128)(2,1)S(1)} %slice.387), channel_id=1, source_target_pairs={{8,0},{16,8},{24,16},{28,24},{20,28},{12,20},{4,12},{0,4},{9,1},{1... | collective-permute-start | bytes 1572872 | tf_op jit(solution)/shard_map/ppermute | solution.py:77
  287.3 42.6 %collective-permute-start.31 = (bf16[256,1024]{1,0:T(8,128)(2,1)S(1)}, bf16[256,1024]{1,0:T(8,128)(2,1)S(1)}, u32[]{:S(2)}, u32[]{:S(2)}) collective-permute-start(bf16[256,1024]{1,0:T(8,128)(2,1)S(1)} %select_convert_fusion.3), channel_id=1, source_target_pairs={{0,2},{2,0},{1,3},{3,1},{4,6},{6,4},{5,7},{7,5},{8,10},{10,8},{9,1... | collective-permute-start | bytes 1572872 | tf_op jit(solution)/shard_map/ppermute | solution.py:16
  288.0 46.6 %collective-permute-start.14 = (bf16[128,512]{1,0:T(8,128)(2,1)S(1)}, bf16[128,512]{1,0:T(8,128)(2,1)S(1)}, u32[]{:S(2)}, u32[]{:S(2)}) collective-permute-start(bf16[128,512]{1,0:T(8,128)(2,1)S(1)} %select_convert_fusion.19), channel_id=1, source_target_pairs={{0,1},{1,0},{2,3},{3,2},{4,5},{5,4},{6,7},{7,6},{8,9},{9,8},{10,11... | collective-permute-start | bytes 393224 | tf_op jit(solution)/shard_map/ppermute | solution.py:16
  317.9 39.8 %collective-permute-start.42 = (bf16[512,1536]{1,0:T(8,128)(2,1)}, bf16[512,1536]{1,0:T(8,128)(2,1)S(1)}, u32[]{:S(2)}, u32[]{:S(2)}) collective-permute-start(bf16[512,1536]{1,0:T(8,128)(2,1)} %collective-permute-done.41), channel_id=1, source_target_pairs={{0,8},{8,16},{16,24},{24,28},{28,20},{20,12},{12,4},{4,0},{1,9},{9... | collective-permute-start | bytes 4718600 | tf_op jit(solution)/shard_map/ppermute | solution.py:72
  318.2 43.9 %collective-permute-start.46 = (bf16[512,1536]{1,0:T(8,128)(2,1)S(1)}, bf16[512,1536]{1,0:T(8,128)(2,1)S(1)}, u32[]{:S(2)}, u32[]{:S(2)}) collective-permute-start(bf16[512,1536]{1,0:T(8,128)(2,1)S(1)} %collective-permute-done.45), channel_id=1, source_target_pairs={{8,0},{16,8},{24,16},{28,24},{20,28},{12,20},{4,12},{0,4},{9,1},{1... | collective-permute-start | bytes 4718600 | tf_op jit(solution)/shard_map/ppermute | solution.py:73
  364.1 57.8 %collective-permute-start.43 = (bf16[512,1536]{1,0:T(8,128)(2,1)S(1)}, bf16[512,1536]{1,0:T(8,128)(2,1)S(1)}, u32[]{:S(2)}, u32[]{:S(2)}) collective-permute-start(bf16[512,1536]{1,0:T(8,128)(2,1)S(1)} %collective-permute-done.42), channel_id=1, source_target_pairs={{0,8},{8,16},{16,24},{24,28},{28,20},{20,12},{12,4},{4,0},{1,9},{9... | collective-permute-start | bytes 4718600 | tf_op jit(solution)/shard_map/ppermute | solution.py:72
  364.7 57.6 %collective-permute-start.47 = (bf16[512,1536]{1,0:T(8,128)(2,1)S(1)}, bf16[512,1536]{1,0:T(8,128)(2,1)S(1)}, u32[]{:S(2)}, u32[]{:S(2)}) collective-permute-start(bf16[512,1536]{1,0:T(8,128)(2,1)S(1)} %collective-permute-done.46), channel_id=1, source_target_pairs={{8,0},{16,8},{24,16},{28,24},{20,28},{12,20},{4,12},{0,4},{9,1},{1... | collective-permute-start | bytes 4718600 | tf_op jit(solution)/shard_map/ppermute | solution.py:73
  388.2 56.3 %collective-permute-start.55 = (bf16[1024,512]{1,0:T(8,128)(2,1)S(1)}, bf16[1024,512]{1,0:T(8,128)(2,1)}, u32[]{:S(2)}, u32[]{:S(2)}) collective-permute-start(bf16[1024,512]{1,0:T(8,128)(2,1)S(1)} %collective-permute-done.51), channel_id=1, source_target_pairs={{0,8},{8,16},{16,24},{24,28},{28,20},{20,12},{12,4},{4,0},{1,9},{9... | collective-permute-start | bytes 3145736 | tf_op jit(solution)/shard_map/ppermute | solution.py:72
  388.5 56.3 %collective-permute-start.56 = (bf16[1024,512]{1,0:T(8,128)(2,1)S(1)}, bf16[1024,512]{1,0:T(8,128)(2,1)}, u32[]{:S(2)}, u32[]{:S(2)}) collective-permute-start(bf16[1024,512]{1,0:T(8,128)(2,1)S(1)} %collective-permute-done.52), channel_id=1, source_target_pairs={{8,0},{16,8},{24,16},{28,24},{20,28},{12,20},{4,12},{0,4},{9,1},{1... | collective-permute-start | bytes 3145736 | tf_op jit(solution)/shard_map/ppermute | solution.py:73
  421.9 39.3 %collective-permute-start.44 = (bf16[256,1536]{1,0:T(8,128)(2,1)S(1)}, bf16[256,1536]{1,0:T(8,128)(2,1)S(1)}, u32[]{:S(2)}, u32[]{:S(2)}) collective-permute-start(bf16[256,1536]{1,0:T(8,128)(2,1)S(1)} %slice.398), channel_id=1, source_target_pairs={{0,8},{8,16},{16,24},{24,28},{28,20},{20,12},{12,4},{4,0},{1,9},{9... | collective-permute-start | bytes 2359304 | tf_op jit(solution)/shard_map/ppermute | solution.py:76
  422.3 39.2 %collective-permute-start.48 = (bf16[256,1536]{1,0:T(8,128)(2,1)S(1)}, bf16[256,1536]{1,0:T(8,128)(2,1)S(1)}, u32[]{:S(2)}, u32[]{:S(2)}) collective-permute-start(bf16[256,1536]{1,0:T(8,128)(2,1)S(1)} %slice.399), channel_id=1, source_target_pairs={{8,0},{16,8},{24,16},{28,24},{20,28},{12,20},{4,12},{0,4},{9,1},{1... | collective-permute-start | bytes 2359304 | tf_op jit(solution)/shard_map/ppermute | solution.py:77
  444.5 60.8 %collective-permute-start.59 = (bf16[1024,512]{1,0:T(8,128)(2,1)}, bf16[1024,512]{1,0:T(8,128)(2,1)}, u32[]{:S(2)}, u32[]{:S(2)}) collective-permute-start(bf16[1024,512]{1,0:T(8,128)(2,1)} %collective-permute-done.55), channel_id=1, source_target_pairs={{0,8},{8,16},{16,24},{24,28},{28,20},{20,12},{12,4},{4,0},{1,9},{9... | collective-permute-start | bytes 3145736 | tf_op jit(solution)/shard_map/ppermute | solution.py:72
  444.7 63.0 %collective-permute-start.60 = (bf16[1024,512]{1,0:T(8,128)(2,1)}, bf16[1024,512]{1,0:T(8,128)(2,1)}, u32[]{:S(2)}, u32[]{:S(2)}) collective-permute-start(bf16[1024,512]{1,0:T(8,128)(2,1)} %collective-permute-done.56), channel_id=1, source_target_pairs={{8,0},{16,8},{24,16},{28,24},{20,28},{12,20},{4,12},{0,4},{9,1},{1... | collective-permute-start | bytes 3145736 | tf_op jit(solution)/shard_map/ppermute | solution.py:73
  (106 other events, 1541.6 us)
